TPU v7x, 32 devices: a whole 2x2x4 slice. The times are simulated.
32 devices in a mesh: view: 8 (over y, x, core), head: 4 (over z).
Axes of the slice: x: 2, y: 2, z: 4, core: 2. Of those that a mesh axis runs over, the one named last changes fastest.
Arguments:
- query: bfloat16 [12288, 3072], P('view', 'head'), may hold values from -180 to 180
- key: bfloat16 [12288, 3072], P('view', 'head'), may hold values from -7 to 7
- value: bfloat16 [12288, 3072], P('view', 'head'), may hold values from -6 to 6
- out_weight: bfloat16 [3072, 3072], P('head'), may hold values from -1.75 to 1.75
- pairs: int32 [8, 7, 4], P('view'), may hold values from 0 to 7, as said below
- counts: int32 [8], replicated, may hold values from 2 to 7, as said below
Outputs:
- mixed: bfloat16 [3072, 12288], P('head', 'view')
Inputs may be any that keep to these rules, and one draw needn't show every extreme that they name: `pairs`: for a view v and a slot s < counts[v], the row (v, a, w, b) has w != v; the list of view w holds (w, b, v, a) among its live slots; two views share at most one pair. Slots from counts[v] on hold (v, 0, v, 0). counts[v] is the number of live slots of view v.
All inputs are finite; a program needn't handle non-finite values.
Results may differ from a plain program's by a relative error of at most 0.017.
Values may be sent and summed in bfloat16 or wider, within the bound.
A program may use at most 128 MiB of HBM per device.

v0:
```python
from functools import partial
import math

import jax
import jax.numpy as jnp
from jax import lax
from jax.sharding import PartitionSpec as P

HEAD_DIM = 128
TILES = 4
TILE = 384


def attend_block(query_tile, key_tile, value_tile, scaling):
    scores = (
        jnp.einsum("qhd,khd->hqk", query_tile, key_tile, preferred_element_type=jnp.float32)
        * scaling
    )
    block_max = scores.max(-1)
    weights = jnp.exp(scores - block_max[..., None])
    block_sum = weights.sum(-1)
    block_acc = jnp.einsum(
        "hqk,khd->qhd", weights.astype(jnp.bfloat16), value_tile, preferred_element_type=jnp.float32
    )
    return (block_max, block_sum, block_acc)


def fold_block(running, block_part):
    run_max, run_sum, run_acc = running
    block_max, block_sum, block_acc = block_part
    joint_max = jnp.maximum(run_max, block_max)
    old_factor = jnp.exp(run_max - joint_max)
    new_factor = jnp.exp(block_max - joint_max)
    joint_sum = run_sum * old_factor + block_sum * new_factor
    joint_acc = run_acc * old_factor.T[..., None] + block_acc * new_factor.T[..., None]
    return (joint_max, joint_sum, joint_acc)


def update_tile(running, tile_index, block_part):
    current = tuple(
        (lax.dynamic_index_in_dim(member, tile_index, 0, keepdims=False) for member in running)
    )
    merged = fold_block(current, block_part)
    return tuple(
        (
            lax.dynamic_update_index_in_dim(member, updated, tile_index, 0)
            for member, updated in zip(running, merged)
        )
    )


def local(query, key, value, out_weight, pairs, counts):
    view_count = lax.axis_size("view")
    myself = lax.axis_index("view")
    tokens, features = query.shape
    local_heads = features // HEAD_DIM
    scaling = 1.0 / math.sqrt(HEAD_DIM)
    tile_query = query.reshape(TILES, TILE, local_heads, HEAD_DIM)
    tile_key = key.reshape(TILES, TILE, local_heads, HEAD_DIM)
    tile_value = value.reshape(TILES, TILE, local_heads, HEAD_DIM)
    slot_rows = pairs[0]
    live_count = lax.dynamic_index_in_dim(counts, myself, 0, keepdims=False)
    live_slots = jnp.arange(slot_rows.shape[0]) < live_count
    own_tiles = slot_rows[:, 1]
    peer_views = slot_rows[:, 2]
    peer_grid = jnp.arange(view_count)
    serve_match = ((peer_views[:, None] == peer_grid[None, :]) & live_slots[:, None]).astype(
        jnp.int32
    )
    wanted = jnp.sum(serve_match * (own_tiles + 1)[:, None], axis=0) - 1
    has_request = wanted >= 0
    source_tiles = jnp.maximum(wanted, 0)
    running = jax.vmap(partial(attend_block, scaling=scaling))(tile_query, tile_key, tile_value)
    stacked = jnp.concatenate(
        [key.reshape(TILES, TILE, features), value.reshape(TILES, TILE, features)], axis=2
    )
    outgoing = jnp.where(
        has_request[:, None, None], stacked[source_tiles], jnp.zeros((), jnp.bfloat16)
    )
    incoming = lax.all_to_all(outgoing, "view", split_axis=0, concat_axis=0, tiled=True)

    def visit_slot(slot_index, carried):
        tile_index = own_tiles[slot_index]
        peer_index = peer_views[slot_index]
        arrived = lax.dynamic_index_in_dim(incoming, peer_index, 0, keepdims=False)
        key_part = arrived[:, :features].reshape(TILE, local_heads, HEAD_DIM)
        value_part = arrived[:, features:].reshape(TILE, local_heads, HEAD_DIM)
        query_part = lax.dynamic_index_in_dim(tile_query, tile_index, 0, keepdims=False)
        return update_tile(
            carried, tile_index, attend_block(query_part, key_part, value_part, scaling)
        )

    running = lax.fori_loop(0, live_count, visit_slot, running)
    final_max, final_sum, final_acc = running
    attended = (
        (final_acc / jnp.transpose(final_sum, (0, 2, 1))[..., None])
        .astype(jnp.bfloat16)
        .reshape(tokens, features)
    )
    return lax.psum_scatter(
        lax.dot_general(
            out_weight, attended, (((0,), (1,)), ((), ())), preferred_element_type=jnp.float32
        ).astype(jnp.bfloat16),
        "head",
        scatter_dimension=0,
        tiled=True,
    )


def solution(mesh):
    placed = (
        P("view", "head"),
        P("view", "head"),
        P("view", "head"),
        P("head", None),
        P("view", None, None),
        P(),
    )
    return jax.shard_map(
        local, mesh=mesh, in_specs=placed, out_specs=P("head", "view"), check_vma=False
    )
```

profile of v0, /device:TPU:0, one launch (start us, length us, event | category | flops | bytes accessed | tf_op | source)
XLA Modules:
  0.0 420.4 jit_solution(15359613827054754061)
XLA Ops:
  6.5 0.8 add_bitcast_fusion
  7.3 1.3 dynamic_slice.29
  8.6 0.6 iota_compare_fusion.1
  9.3 4.8 %pad_maximum_fusion = bf16[4,384,1536]{2,1,0:T(8,128)(2,1)} fusion(bf16[4,384,768]{2,1,0:T(8,128)(2,1)} %bitcast.112, bf16[4,384,768]{2,1,0:T(8,128)(2,1)} %bitcast.111), kind=kLoop, calls=%fused_computation.44 | loop fusion | flops 9437184 | bytes 9437184 | tf_op jit(solution)/shard_map/concatenate | solution.py:74
  14.2 7.4 %gather_fusion = bf16[8,384,1536]{2,1,0:T(8,128)(2,1)} fusion(bf16[4,384,1536]{2,1,0:T(8,128)(2,1)} %pad_maximum_fusion, s32[1024]{0:T(1024)S(1)} %pad_clamp_fusion), kind=kCustom, calls=%fused_computation | custom fusion | bytes 18874400 | tf_op jit(solution)/shard_map/gather | solution.py:78
  21.6 7.9 %broadcast_select_fusion = bf16[8,384,1536]{2,1,0:T(8,128)(2,1)} fusion(bf16[8,384,1536]{2,1,0:T(8,128)(2,1)} %gather_fusion, pred[8]{0:T(512)(128)(4,1)S(1)} %add_compare_fusion), kind=kLoop, calls=%fused_computation.40 | loop fusion | flops 4718592 | bytes 18874376 | tf_op jit(solution)/shard_map/jit(_where)/select_n | solution.py:77
  29.5 5.2 %all-to-all-start = ((bf16[8,384,1536]{2,1,0:T(8,128)(2,1)}), bf16[8,384,1536]{2,1,0:T(8,128)(2,1)}, u32[]{:S(2)}, u32[]{:S(2)}) async-start(bf16[8,384,1536]{2,1,0:T(8,128)(2,1)} %broadcast_select_fusion), calls=%async_computation | async-start | bytes 18874368 | tf_op jit(solution)/shard_map/all_to_all | solution.py:80
  34.7 4.8 %reshape.69 = bf16[4,384,6,128]{3,2,1,0:T(8,128)(2,1)S(1)} reshape(bf16[1536,768]{1,0:T(8,128)(2,1)} %param.9) | data formatting | bytes 4718592 | tf_op jit(solution)/shard_map/reshape | solution.py:59
  39.5 6.0 %reshape.70 = bf16[4,384,6,128]{3,2,1,0:T(8,128)(2,1)} reshape(bf16[1536,768]{1,0:T(8,128)(2,1)} %param.10) | data formatting | bytes 4718592 | tf_op jit(solution)/shard_map/reshape | solution.py:60
  45.5 6.0 %reshape.71 = bf16[4,384,6,128]{3,2,1,0:T(8,128)(2,1)} reshape(bf16[1536,768]{1,0:T(8,128)(2,1)} %param.8) | data formatting | bytes 4718592 | tf_op jit(solution)/shard_map/reshape | solution.py:58
  51.5 2.4 copy.31
  54.0 6.4 %multiply_reduce_fusion.1 = (f32[4,6,384]{2,1,0:T(8,128)S(1)}, f32[4,6,384,384]{2,3,1,0:T(8,128)}) fusion(bf16[4,384,6,128]{3,1,2,0:T(8,128)(2,1)S(1)} %copy.31, bf16[4,384,6,128]{3,2,1,0:T(8,128)(2,1)S(1)} %reshape.69), kind=kOutput, calls=%fused_computation.35 | convolution fusion | flops 913038336 | bytes 18911232 | tf_op jit(solution)/shard_map/vmap(qhd,khd->hqk)/dot_general | solution.py:16
  60.3 11.4 %fusion.44 = f32[4,384,6,128]{3,1,2,0:T(8,128)} fusion(bf16[4,384,6,128]{3,2,1,0:T(8,128)(2,1)} %reshape.70, f32[4,6,384,384]{2,3,1,0:T(8,128)} %get-tuple-element.113, f32[4,6,384]{2,1,0:T(8,128)S(1)} %get-tuple-element.187), kind=kOutput, calls=%fused_computation.49 | convolution fusion | flops 916586496 | bytes 21270528 | tf_op jit(solution)/shard_map/vmap(hqk,khd->qhd)/dot_general | solution.py:22
  71.7 6.1 %copy.36 = f32[4,384,6,128]{1,3,2,0:T(8,128)} copy(f32[4,384,6,128]{3,1,2,0:T(8,128)} %fusion.44) | data formatting | bytes 9437184 | tf_op jit(solution)/shard_map/while | solution.py:93
  77.8 7.4 %fusion.35 = f32[4,6,384]{2,1,0:T(8,128)S(1)} fusion(f32[4,6,384,384]{2,3,1,0:T(8,128)} %get-tuple-element.113, f32[4,6,384]{2,1,0:T(8,128)S(1)} %get-tuple-element.187), kind=kLoop, calls=%fused_computation.37 | loop fusion | flops 10607616 | bytes 14229504 | tf_op jit(solution)/shard_map/vmap()/reduce_sum | solution.py:21
  85.2 55.2 %all-to-all-done = bf16[8,384,1536]{2,1,0:T(8,128)(2,1)} async-done(((bf16[8,384,1536]{2,1,0:T(8,128)(2,1)}), bf16[8,384,1536]{2,1,0:T(8,128)(2,1)}, u32[]{:S(2)}, u32[]{:S(2)}) %all-to-all-start) | async-done | bytes 9437216 | tf_op jit(solution)/shard_map/all_to_all | solution.py:80
  140.4 54.8 %while.14 = (s32[]{:T(128)}, f32[4,6,384]{2,1,0:T(8,128)S(1)}, f32[4,6,384]{2,1,0:T(8,128)S(1)}, f32[4,384,6,128]{1,3,2,0:T(8,128)}, s32[]{:T(128)}, /*index=5*/...) while((s32[]{:T(128)}, f32[4,6,384]{2,1,0:T(8,128)S(1)}, ...), condition=%wide.region_6.7_spmd, body=%wide.region_3.6_spmd.sunk | while | flops 460963584 | bytes 24348964 | solution.py:93
  141.3 0.6 dynamic_slice.58
  143.8 1.4 constant_dynamic-slice_fusion.4
  145.1 0.7 copy.61
  146.0 0.6 dynamic_slice.57
  148.5 1.7 multiply_reduce_fusion.3
  150.9 1.4 constant_dynamic-slice_fusion.5
  152.2 1.9 fusion.72
  154.8 0.6 dynamic_slice.58
  157.3 1.4 constant_dynamic-slice_fusion.4
  158.6 0.7 copy.61
  159.5 0.6 dynamic_slice.57
  162.0 1.7 multiply_reduce_fusion.3
  164.4 1.4 constant_dynamic-slice_fusion.5
  165.7 1.9 fusion.72
  170.8 1.4 constant_dynamic-slice_fusion.4
  172.1 0.7 copy.61
  173.0 0.6 dynamic_slice.57
  175.5 1.7 multiply_reduce_fusion.3
  177.9 1.4 constant_dynamic-slice_fusion.5
  179.3 1.9 fusion.72
  184.3 1.4 constant_dynamic-slice_fusion.4
  185.6 0.7 copy.61
  186.5 0.6 dynamic_slice.57
  189.0 1.7 multiply_reduce_fusion.3
  191.4 1.4 constant_dynamic-slice_fusion.5
  192.8 1.9 fusion.72
  195.3 3.0 divide_convert_fusion
  198.4 1.8 copy.39
  200.6 9.9 %fusion.36 = bf16[3072,1536]{0,1:T(8,128)(2,1)} fusion(bf16[1536,768]{0,1:T(8,128)(2,1)S(1)} %bitcast.113, bf16[768,3072]{1,0:T(8,128)(2,1)S(1)} %bitcast.117), kind=kOutput, calls=%fused_computation.39 | convolution fusion | flops 7252475904 | bytes 16515072 | tf_op jit(solution)/shard_map/dot_general | solution.py:101
  210.5 198.8 %reduce-scatter.2.cloned.1.call-done = bf16[768,1536]{0,1:T(8,128)(2,1)} async-done(((bf16[3072,1536]{0,1:T(8,128)(2,1)}), bf16[768,1536]{0,1:T(8,128)(2,1)}) %reduce-scatter.2.cloned.1.call-update) | async-done | bytes 2359312 | tf_op jit(solution)/shard_map/reduce_scatter | solution.py:100
  409.3 4.3 %copy.40 = bf16[768,1536]{1,0:T(8,128)(2,1)} copy(bf16[768,1536]{0,1:T(8,128)(2,1)} %reduce-scatter.2.cloned.1.call-done) | data formatting | bytes 4718592 | tf_op jit(solution)/shard_map/reduce_scatter | solution.py:100
  (32 shorter events, 4.8 us)
Async XLA Ops:
  29.5 110.9 %all-to-all-start = ((bf16[8,384,1536]{2,1,0:T(8,128)(2,1)}), bf16[8,384,1536]{2,1,0:T(8,128)(2,1)}, u32[]{:S(2)}, u32[]{:S(2)}) async-start(bf16[8,384,1536]{2,1,0:T(8,128)(2,1)} %broadcast_select_fusion), calls=%async_computation | async-start | bytes 18874368 | tf_op jit(solution)/shard_map/all_to_all | solution.py:80
  34.7 374.6 %reduce-scatter.2.cloned.1.call-start = ((), (), s32[]{:S(2)}) async-start(), calls=%async_computation.2 | async-start | bytes 11796480 | tf_op jit(solution)/shard_map/reduce_scatter | solution.py:100
  53.9 6.4 %copy-start = (bf16[4,384,6,128]{3,1,2,0:T(8,128)(2,1)}, bf16[4,384,6,128]{3,1,2,0:T(8,128)(2,1)S(1)}, u32[]{:S(2)}) copy-start(bf16[4,384,6,128]{3,1,2,0:T(8,128)(2,1)S(1)} %copy.31) | copy-start | bytes 7077892
  195.3 5.3 %slice-start = ((s8[4718592]{0:T(1024)(128)(4,1)}), s8[4194304]{0:T(1024)(128)(4,1)S(1)}, s32[]{:S(2)}) async-start(s8[4718592]{0:T(1024)(128)(4,1)} %bitcast.116), calls=%async_computation.3 | async-start | bytes 8388608
  198.3 2.3 slice-start.1
Sparse Core Ops, SparseCore 0:
  210.7 198.5 reduce-scatter.1
where the time goes:
time: 424 us; the launch traced here: 420 us
  waiting for transfers between devices  254 us (60%)
  local copies, waits for them, and re-layouts  59.6 us (14%)
  matrix products  42.2 us (10%)
  other arithmetic  27.2 us (6%)
  loops' own time  18.6 us (4%)
  between operations  13.5 us (3%)
  starting transfers between devices  5.21 us (1%)
    reduce_scatter x1, waiting for transfers between devices, local(): lax.psum_scatter(lax.dot_general(out_weight, attended, (((0,), (1,)), (()...  199 us
    all_to_all x1, waiting for transfers between devices, local(): lax.all_to_all(outgoing, 'view', split_axis=0, concat_axis=0, tiled=True)  55.2 us
    dot_general x5, matrix products, attend_block(): jnp.einsum('hqk,khd->qhd', weights.astype(jnp.bfloat16), value_tile, pref...  19 us
    another operation x1, loops' own time, local(): running = lax.fori_loop(0, live_count, visit_slot, running)  18.6 us
    dot_general x5, matrix products, attend_block(): jnp.einsum('qhd,khd->hqk', query_tile, key_tile, preferred_element_type=j...  13.3 us
    dot_general x1, matrix products, local(): lax.dot_general(out_weight, attended, (((0,), (1,)), ((), ())), preferred...  9.9 us
    reduce_sum x5, other arithmetic, attend_block(): block_sum = weights.sum(-1)  9.75 us
  transfers between devices with their start and end apart: 2, of which 2 were waited for; matrix products, arithmetic and copies ran while one was open for 12% of the time, Pallas kernels for 0%

commit v1 on v0

v1 whole, which is shorter than its diff:
```python
import functools
import math

import jax
import jax.numpy as jnp
from jax import lax
from jax.experimental import pallas as pl
from jax.experimental.pallas import tpu as pltpu
from jax.sharding import PartitionSpec as P

HEAD_DIM = 128
TILES = 4
SCALE = math.log2(math.e) / math.sqrt(HEAD_DIM)


def collect_kernel(source_ref, key_ref, value_ref, out_ref):
    width = key_ref.shape[1]
    out_ref[0, :, :width] = key_ref[...]
    out_ref[0, :, width:] = value_ref[...]


def collect(source_tiles, key, value, chunk, width):
    views = source_tiles.shape[0]
    tile = key.shape[0] // TILES
    rows = pl.BlockSpec((tile, width), lambda p, source: (source[p], chunk))
    return pl.pallas_call(
        collect_kernel,
        grid_spec=pltpu.PrefetchScalarGridSpec(
            num_scalar_prefetch=1,
            grid=(views,),
            in_specs=[rows, rows],
            out_specs=pl.BlockSpec((1, tile, 2 * width), lambda p, source: (p, 0, 0)),
        ),
        out_shape=jax.ShapeDtypeStruct((views, tile, 2 * width), key.dtype),
        compiler_params=pltpu.CompilerParams(vmem_limit_bytes=16 * 2**20),
        cost_estimate=pl.CostEstimate(
            flops=0, bytes_accessed=views * tile * width * 8, transcendentals=0
        ),
    )(source_tiles, key, value)


def block_scores(key_tile, query_tile):
    return lax.dot_general(
        key_tile, query_tile, (((1,), (1,)), ((), ())), preferred_element_type=jnp.float32
    )


def block_values(value_tile, weights):
    return lax.dot_general(
        value_tile,
        weights.astype(jnp.bfloat16),
        (((0,), (0,)), ((), ())),
        preferred_element_type=jnp.float32,
    )


def attend_kernel(
    slots, tile, meta_ref, q_ref, k_ref, v_ref, pk_ref, pv_ref, out_ref, m_ref, l_ref, acc_ref
):
    for t in range(TILES):
        rows = pl.ds(t * tile, tile)
        scores = block_scores(k_ref[rows, :], q_ref[rows, :])
        top = jnp.max(scores, axis=0, keepdims=True)
        weights = jnp.exp2((scores - top) * SCALE)
        m_ref[t] = top
        l_ref[t] = jnp.sum(weights, axis=0, keepdims=True)
        acc_ref[t] = block_values(v_ref[rows, :], weights)

    def visit(slot, carry):
        t = meta_ref[1 + slot]
        peer = meta_ref[1 + slots + slot]
        rows = pl.ds(pl.multiple_of(t * tile, tile), tile)
        scores = block_scores(pk_ref[peer], q_ref[rows, :])
        old = m_ref[t]
        top = jnp.maximum(old, jnp.max(scores, axis=0, keepdims=True))
        weights = jnp.exp2((scores - top) * SCALE)
        factor = jnp.exp2((old - top) * SCALE)
        m_ref[t] = top
        l_ref[t] = l_ref[t] * factor + jnp.sum(weights, axis=0, keepdims=True)
        acc_ref[t] = acc_ref[t] * factor + block_values(pv_ref[peer], weights)
        return carry

    lax.fori_loop(0, meta_ref[0], visit, 0)
    for t in range(TILES):
        out_ref[:, pl.ds(t * tile, tile)] = (acc_ref[t] / l_ref[t]).astype(out_ref.dtype)


def attend(meta, query, key, value, incoming, chunk, heads):
    tokens = query.shape[0]
    tile = tokens // TILES
    views = incoming.shape[0]
    slots = (meta.shape[0] - 1) // 2
    own = pl.BlockSpec((tokens, HEAD_DIM), lambda h, meta: (0, chunk * heads + h))
    peer_key = pl.BlockSpec((views, tile, HEAD_DIM), lambda h, meta: (0, 0, h))
    peer_value = pl.BlockSpec((views, tile, HEAD_DIM), lambda h, meta: (0, 0, heads + h))
    blocks = heads * (TILES + min(slots, 7)) * tile * tile
    return pl.pallas_call(
        functools.partial(attend_kernel, slots, tile),
        grid_spec=pltpu.PrefetchScalarGridSpec(
            num_scalar_prefetch=1,
            grid=(heads,),
            in_specs=[own, own, own, peer_key, peer_value],
            out_specs=pl.BlockSpec((HEAD_DIM, tokens), lambda h, meta: (h, 0)),
            scratch_shapes=[
                pltpu.VMEM((TILES, 1, tile), jnp.float32),
                pltpu.VMEM((TILES, 1, tile), jnp.float32),
                pltpu.VMEM((TILES, HEAD_DIM, tile), jnp.float32),
            ],
        ),
        out_shape=jax.ShapeDtypeStruct((heads * HEAD_DIM, tokens), query.dtype),
        compiler_params=pltpu.CompilerParams(vmem_limit_bytes=40 * 2**20),
        cost_estimate=pl.CostEstimate(
            flops=blocks * HEAD_DIM * 8,
            bytes_accessed=heads * HEAD_DIM * (8 * tokens + 4 * views * tile),
            transcendentals=blocks,
        ),
    )(meta, query, key, value, incoming, incoming)


def local(query, key, value, out_weight, pairs, counts):
    views = lax.axis_size("view")
    groups = lax.axis_size("head")
    me = lax.axis_index("view")
    features = query.shape[1]
    heads = features // HEAD_DIM
    chunks = 3 if heads % 3 == 0 else 1
    per = heads // chunks
    width = per * HEAD_DIM

    slot_rows = pairs[0]
    live_count = lax.dynamic_index_in_dim(counts, me, 0, keepdims=True)
    live = jnp.arange(slot_rows.shape[0]) < live_count
    own_tiles, peers = slot_rows[:, 1], slot_rows[:, 2]
    match = (peers[:, None] == jnp.arange(views)[None, :]) & live[:, None]
    source_tiles = jnp.sum(jnp.where(match, own_tiles[:, None], 0), axis=0)
    meta = jnp.concatenate([live_count, own_tiles, peers])

    incoming = [
        lax.all_to_all(
            collect(source_tiles, key, value, c, width), "view", 0, 0, tiled=True
        )
        for c in range(chunks)
    ]
    share = features // views
    mine = lax.dynamic_slice_in_dim(out_weight, me * share, share, 0)
    mine = lax.all_to_all(
        mine.reshape(share, groups, -1), "head", split_axis=1, concat_axis=1, tiled=True
    )
    weight = lax.all_gather(mine, "view", axis=0, tiled=True)

    total = None
    for c in range(chunks):
        attended = attend(meta, query, key, value, incoming[c], c, per)
        gathered = lax.all_gather(attended, "head", axis=0, tiled=False)
        gathered = gathered.reshape(groups * width, -1)
        part = jnp.swapaxes(weight[c * width : (c + 1) * width], 0, 1)
        term = lax.dot_general(
            part.reshape(groups * width, -1),
            gathered,
            (((0,), (0,)), ((), ())),
            preferred_element_type=jnp.float32,
        )
        total = term if total is None else total + term
    return total.astype(jnp.bfloat16)


def solution(mesh):
    placed = (
        P("view", "head"),
        P("view", "head"),
        P("view", "head"),
        P("head", None),
        P("view", None, None),
        P(),
    )
    return jax.shard_map(
        local, mesh=mesh, in_specs=placed, out_specs=P("head", "view"), check_vma=False
    )
```

time: 424 us -> 317 us (0.75)
  waiting for transfers between devices: 254 us -> 101 us
  blocking collectives: 0 us -> 104 us
  Pallas kernels: 0 us -> 42 us
  local copies, waits for them, and re-layouts: 59.6 us -> 27.6 us
  other arithmetic: 27.2 us -> 1.43 us
  matrix products: 42.2 us -> 21.8 us
  loops' own time: 18.6 us -> 0 us
    reduce_scatter x1 -> x0, waiting for transfers between devices: 199 us -> none  [local(): lax.psum_scatter(lax.dot_general(out_weight, attended, (((0,), (1,)), (()...]
    all_to_all x0 -> x3, blocking collectives: none -> 104 us  [the longest x2 81.9 us: local(): lax.all_to_all(collect(source_tiles, key, value, c, width), 'view', 0, 0,...]
    all_gather x0 -> x4, waiting for transfers between devices: none -> 49.4 us  [the longest x3 49.4 us: local(): gathered = lax.all_gather(attended, 'head', axis=0, tiled=False)]
    pallas_call x0 -> x6, Pallas kernels: none -> 42 us  [the longest x3 38.4 us: attend(): pl.pallas_call(functools.partial(attend_kernel, slots, tile), grid_spec=p...]
    dot_general x11 -> x3, matrix products: 42.2 us -> 21.8 us  [local(): lax.dot_general(part.reshape(groups * width, -1), gathered, (((0,), (0,))...]
    unnamed x7 -> x31, local copies, waits for them, and re-layouts: 0.42 us -> 20 us
    reshape x4 -> x1, local copies, waits for them, and re-layouts: 19.2 us -> 0.04 us  [local(): mine.reshape(share, groups, -1)]
    another operation x1 -> x0, loops' own time: 18.6 us -> none  [local(): running = lax.fori_loop(0, live_count, visit_slot, running)]
  transfers between devices with their start and end apart: 2 -> 5, of which waited for: 2 -> 2; matrix products, arithmetic and copies ran while one was open for 12% -> 10% of each run, Pallas kernels for 0% -> 13%
where the time goes in v1:
time: 317 us; the launch traced here: 316 us
  blocking collectives  104 us (33%)
  waiting for transfers between devices  101 us (32%)
  Pallas kernels  42 us (13%)
  local copies, waits for them, and re-layouts  27.6 us (9%)
  matrix products  21.8 us (7%)
  between operations  13.3 us (4%)
  starting transfers between devices  4.58 us (1%)
    all_to_all x2, blocking collectives, local(): lax.all_to_all(collect(source_tiles, key, value, c, width), 'view', 0, 0,...  81.9 us
    all_to_all x1, waiting for transfers between devices, local(): lax.all_to_all(collect(source_tiles, key, value, c, width), 'view', 0, 0,...  51.9 us
    all_gather x3, waiting for transfers between devices, local(): gathered = lax.all_gather(attended, 'head', axis=0, tiled=False)  49.4 us
    pallas_call x3, Pallas kernels, attend(): pl.pallas_call(functools.partial(attend_kernel, slots, tile), grid_spec=p...  38.4 us
    all_to_all x1, blocking collectives, local(): lax.all_to_all(mine.reshape(share, groups, -1), 'head', split_axis=1, con...  22 us
    dot_general x3, matrix products, local(): lax.dot_general(part.reshape(groups * width, -1), gathered, (((0,), (0,))...  21.8 us
    unnamed x31, local copies, waits for them, and re-layouts  20 us
  transfers between devices with their start and end apart: 5, of which 2 were waited for; matrix products, arithmetic and copies ran while one was open for 10% of the time, Pallas kernels for 13%

profile of v1, /device:TPU:0, one launch (start us, length us, event | category | flops | bytes accessed | tf_op | source)
XLA Modules:
  0.0 316.0 jit_solution(16335243854851760745)
XLA Ops:
  6.5 0.0 all-gather.8.cloned.1.call-start
  6.5 1.3 constant_dynamic-slice_fusion
  7.8 22.0 %all_to_all.20 = bf16[96,4,768]{2,0,1:T(8,128)(2,1)S(1)} all-to-all(bf16[96,4,768]{2,0,1:T(8,128)(2,1)S(1)} %bitcast.36), channel_id=1, replica_groups=mesh['view'=8,'head'=4] {'head'}, dimensions={1} | all-to-all | bytes 1179648 | tf_op jit(solution)/shard_map/all_to_all | solution.py:146
  29.9 1.3 copy.18
  31.1 0.0 all-gather.8.cloned.1.call-update
  31.2 0.0 copy-done.13
  31.2 0.7 dynamic_slice.8
  31.8 0.6 iota_compare_fusion.1
  32.5 0.1 select_reduce_fusion.source_ref
  32.6 0.0 copy-start.1
  32.6 1.7 copy-done.1
  34.3 1.2 shard_map.64
  35.5 1.8 copy-done.10
  37.2 4.5 %all-to-all-start.1 = ((bf16[8,384,512]{2,1,0:T(8,128)(2,1)}), bf16[8,384,512]{2,1,0:T(8,128)(2,1)}, u32[]{:S(2)}, u32[]{:S(2)}) async-start(bf16[8,384,512]{2,1,0:T(8,128)(2,1)} %copy-done.10), calls=%async_computation.1 | async-start | bytes 6291456 | tf_op jit(solution)/shard_map/all_to_all | solution.py:139
  41.7 0.0 all-gather.10.cloned.1.call-start
  41.7 0.7 pad_add_fusion.meta_ref
  42.4 51.9 %all-to-all-done.1.pk_ref.pv_ref = bf16[8,384,512]{2,1,0:T(8,128)(2,1)} async-done(((bf16[8,384,512]{2,1,0:T(8,128)(2,1)}), bf16[8,384,512]{2,1,0:T(8,128)(2,1)}, u32[]{:S(2)}, u32[]{:S(2)}) %all-to-all-start.1) | async-done | bytes 3145760 | tf_op jit(solution)/shard_map/all_to_all | solution.py:139
  94.4 1.7 copy-done.2
  96.0 1.7 copy-done.7
  97.7 13.2 %shard_map.65 = bf16[256,1536]{1,0:T(8,128)(2,1)} custom-call(s32[15]{0:T(128)S(1)} %pad_add_fusion.meta_ref, bf16[1536,768]{1,0:T(8,128)(2,1)S(1)} %copy-done.7, bf16[1536,768]{1,0:T(8,128)(2,1)S(1)} %copy-done, bf16[1536,768]{1,0:T(8,128)(2,1)S(1)} %copy-done.2, bf16[8,384,512]{2,1,0:T(8,128)(2,1)} %all-to-all-done.1.pk_ref.pv_ref, ...), custom_call_target="tpu_custom_call" | custom-call | flops 3321888768 | bytes 6291456 | tf_op jit(solution)/shard_map/pallas_call | solution.py:97
  110.9 0.0 all-gather.10.cloned.1.call-update
  111.0 0.0 all-gather.12.cloned.1.call-start
  111.0 0.0 copy-start.3
  111.0 1.7 copy-done.3
  112.7 1.2 shard_map.66
  113.9 0.0 copy-start.4
  113.9 0.0 copy-start.8
  113.9 41.0 %all_to_all.21.pk_ref.pv_ref = bf16[8,384,512]{2,1,0:T(8,128)(2,1)S(1)} all-to-all(bf16[8,384,512]{2,1,0:T(8,128)(2,1)S(1)} %shard_map.66), channel_id=1, replica_groups=mesh['view'=8,'head'=4] {'view'}, dimensions={0} | all-to-all | bytes 6291456 | tf_op jit(solution)/shard_map/all_to_all | solution.py:139
  154.9 12.6 %shard_map.67 = bf16[256,1536]{1,0:T(8,128)(2,1)} custom-call(s32[15]{0:T(128)S(1)} %pad_add_fusion.meta_ref, bf16[1536,768]{1,0:T(8,128)(2,1)S(1)} %copy-done.8, bf16[1536,768]{1,0:T(8,128)(2,1)S(1)} %copy-done, bf16[1536,768]{1,0:T(8,128)(2,1)S(1)} %copy-done.4, bf16[8,384,512]{2,1,0:T(8,128)(2,1)S(1)} %all_to_all.21.pk_ref.pv_ref, ...), custom_call_target="tpu_custom_call" | custom-call | flops 3321888768 | bytes 6291456 | tf_op jit(solution)/shard_map/pallas_call | solution.py:97
  167.5 0.0 all-gather.12.cloned.1.call-update
  167.5 0.0 all-gather.14.cloned.1.call-start
  167.5 0.0 copy-start.5
  167.5 1.7 copy-done.5
  169.2 1.2 shard_map.68
  170.4 0.0 copy-start.6
  170.4 0.0 copy-start.9
  170.4 40.9 %all_to_all.22.pk_ref.pv_ref = bf16[8,384,512]{2,1,0:T(8,128)(2,1)S(1)} all-to-all(bf16[8,384,512]{2,1,0:T(8,128)(2,1)S(1)} %shard_map.68), channel_id=1, replica_groups=mesh['view'=8,'head'=4] {'view'}, dimensions={0} | all-to-all | bytes 6291456 | tf_op jit(solution)/shard_map/all_to_all | solution.py:139
  211.3 12.6 %shard_map.69 = bf16[256,1536]{1,0:T(8,128)(2,1)} custom-call(s32[15]{0:T(128)S(1)} %pad_add_fusion.meta_ref, bf16[1536,768]{1,0:T(8,128)(2,1)S(1)} %copy-done.9, bf16[1536,768]{1,0:T(8,128)(2,1)S(1)} %copy-done, bf16[1536,768]{1,0:T(8,128)(2,1)S(1)} %copy-done.6, bf16[8,384,512]{2,1,0:T(8,128)(2,1)S(1)} %all_to_all.22.pk_ref.pv_ref, ...), custom_call_target="tpu_custom_call" | custom-call | flops 3321888768 | bytes 6291456 | tf_op jit(solution)/shard_map/pallas_call | solution.py:97
  223.9 0.0 all-gather.14.cloned.1.call-update
  224.0 0.0 all-gather.8.cloned.1.call-done
  224.0 4.4 %fusion.7 = (bf16[256,4,768]{2,1,0:T(4,128)(2,1)S(1)}, bf16[256,4,768]{2,1,0:T(4,128)(2,1)}, bf16[256,4,768]{2,1,0:T(4,128)(2,1)}) fusion(bf16[768,4,768]{2,1,0:T(4,128)(2,1)} %all-gather.8.cloned.1.call-done), kind=kLoop, calls=%fused_computation.17 | loop fusion | bytes 9437184 | tf_op jit(solution)/shard_map/slice | solution.py:156
  228.4 3.8 %copy.22 = bf16[256,4,768]{0,2,1:T(8,128)(2,1)} copy(bf16[256,4,768]{2,1,0:T(4,128)(2,1)} %get-tuple-element.7) | data formatting | bytes 3145728
  232.1 3.8 %copy.23 = bf16[256,4,768]{0,2,1:T(8,128)(2,1)} copy(bf16[256,4,768]{2,1,0:T(4,128)(2,1)} %get-tuple-element.6) | data formatting | bytes 3145728
  235.9 2.3 copy.24
  238.3 7.1 %fusion.4 = f32[768,1536,1]{1,0,2:T(8,128)} fusion(bf16[4,256,1536]{2,1,0:T(8,128)(2,1)} %bitcast.38, bf16[256,4,768]{0,2,1:T(8,128)(2,1)} %copy.22), kind=kOutput, calls=%fused_computation.6 | convolution fusion | flops 2415919104 | bytes 9437184 | tf_op jit(solution)/shard_map/dot_general | solution.py:157
  245.4 7.6 %fusion.2 = f32[768,1536,1]{1,0,2:T(8,128)} fusion(bf16[4,256,1536]{2,1,0:T(8,128)(2,1)} %bitcast.39, bf16[256,4,768]{0,2,1:T(8,128)(2,1)} %copy.23), kind=kOutput, calls=%fused_computation.4 | convolution fusion | flops 2415919104 | bytes 9437184 | tf_op jit(solution)/shard_map/dot_general | solution.py:157
  253.0 49.4 %all-gather.14.cloned.1.call-done = bf16[1024,1536]{1,0:T(8,128)(2,1)} async-done(((bf16[256,1536]{1,0:T(8,128)(2,1)}), bf16[1024,1536]{1,0:T(8,128)(2,1)}) %all-gather.14.cloned.1.call-update) | async-done | bytes 3145744 | tf_op jit(solution)/shard_map/all_gather | solution.py:154
  302.3 7.1 %fusion = bf16[768,1536]{1,0:T(8,128)(2,1)} fusion(f32[768,1536,1]{1,0,2:T(8,128)} %fusion.2, f32[768,1536,1]{1,0,2:T(8,128)} %fusion.4, bf16[4,256,1536]{2,1,0:T(8,128)(2,1)} %bitcast.40, bf16[256,4,768]{0,2,1:T(8,128)(2,1)S(1)} %copy-done.11), kind=kOutput, calls=%fused_computation.1 | convolution fusion | flops 2419458048 | bytes 16515072 | tf_op jit(solution)/shard_map/dot_general | solution.py:157
  (18 shorter events, 0.1 us)
Async XLA Ops:
  6.5 24.6 %copy-start.13 = (s32[8]{0:T(128)S(1)}, s32[8]{0:T(128)}, u32[]{:S(2)}) copy-start(s32[8]{0:T(128)} %param.11) | copy-start | bytes 100
  6.5 25.9 %copy-start.12 = (s32[1,7,4]{1,2,0:T(4,128)S(1)}, s32[1,7,4]{1,2,0:T(4,128)}, u32[]{:S(2)}) copy-start(s32[1,7,4]{1,2,0:T(4,128)} %param.10) | copy-start | bytes 340
  6.5 26.0 %copy-start = (bf16[1536,768]{1,0:T(8,128)(2,1)S(1)}, bf16[1536,768]{1,0:T(8,128)(2,1)}, u32[]{:S(2)}) copy-start(bf16[1536,768]{1,0:T(8,128)(2,1)} %k_ref.5) | copy-start | bytes 7077892
  6.5 217.4 %all-gather.8.cloned.1.call-start = ((), (), s32[]{:S(2)}) async-start(), calls=%async_computation.4 | async-start | bytes 5308416 | tf_op jit(solution)/shard_map/all_gather | solution.py:149
  32.6 1.7 copy-start.1
  35.4 1.8 copy-start.10
  37.2 57.2 %all-to-all-start.1 = ((bf16[8,384,512]{2,1,0:T(8,128)(2,1)}), bf16[8,384,512]{2,1,0:T(8,128)(2,1)}, u32[]{:S(2)}, u32[]{:S(2)}) async-start(bf16[8,384,512]{2,1,0:T(8,128)(2,1)} %copy-done.10), calls=%async_computation.1 | async-start | bytes 6291456 | tf_op jit(solution)/shard_map/all_to_all | solution.py:139
  41.7 196.6 %all-gather.10.cloned.1.call-start = ((), (), s32[]{:S(2)}) async-start(), calls=%async_computation.5 | async-start | bytes 3932160 | tf_op jit(solution)/shard_map/all_gather | solution.py:154
  94.4 1.7 copy-start.2
  96.0 1.7 copy-start.7
  111.0 134.4 %all-gather.12.cloned.1.call-start = ((), (), s32[]{:S(2)}) async-start(), calls=%async_computation.6 | async-start | bytes 3932160 | tf_op jit(solution)/shard_map/all_gather | solution.py:154
  111.0 1.7 copy-start.3
  113.9 41.0 %copy-start.4 = (bf16[1536,768]{1,0:T(8,128)(2,1)S(1)}, bf16[1536,768]{1,0:T(8,128)(2,1)}, u32[]{:S(2)}) copy-start(bf16[1536,768]{1,0:T(8,128)(2,1)} %v_ref.5) | copy-start | bytes 7077892
  113.9 41.0 %copy-start.8 = (bf16[1536,768]{1,0:T(8,128)(2,1)S(1)}, bf16[1536,768]{1,0:T(8,128)(2,1)}, u32[]{:S(2)}) copy-start(bf16[1536,768]{1,0:T(8,128)(2,1)} %q_ref.5) | copy-start | bytes 7077892
  167.5 134.8 %all-gather.14.cloned.1.call-start = ((), (), s32[]{:S(2)}) async-start(), calls=%async_computation.7 | async-start | bytes 3932160 | tf_op jit(solution)/shard_map/all_gather | solution.py:154
  167.5 1.7 copy-start.5
  170.4 40.9 %copy-start.6 = (bf16[1536,768]{1,0:T(8,128)(2,1)S(1)}, bf16[1536,768]{1,0:T(8,128)(2,1)}, u32[]{:S(2)}) copy-start(bf16[1536,768]{1,0:T(8,128)(2,1)} %v_ref.5) | copy-start | bytes 7077892
  170.4 40.9 %copy-start.9 = (bf16[1536,768]{1,0:T(8,128)(2,1)S(1)}, bf16[1536,768]{1,0:T(8,128)(2,1)}, u32[]{:S(2)}) copy-start(bf16[1536,768]{1,0:T(8,128)(2,1)} %q_ref.5) | copy-start | bytes 7077892
  245.4 57.0 %copy-start.11 = (bf16[256,4,768]{0,2,1:T(8,128)(2,1)S(1)}, bf16[256,4,768]{0,2,1:T(8,128)(2,1)}, u32[]{:S(2)}) copy-start(bf16[256,4,768]{0,2,1:T(8,128)(2,1)} %copy.24) | copy-start | bytes 4718596
Sparse Core Ops, SparseCore 0:
  31.3 63.5 all-gather.7
  111.1 63.8 all-gather.9
  176.5 62.1 all-gather.11
  240.1 62.1 all-gather.13

commit v2 on v1

--- a/solution.py
+++ b/solution.py
@@ -117,13 +117,39 @@
     )(meta, query, key, value, incoming, incoming)
 
 
+def shift(array, axis, step):
+    size = lax.axis_size(axis)
+    return lax.ppermute(array, axis, [(i, (i + step) % size) for i in range(size)])
+
+
+def spread_weight(out_weight, after):
+    views, groups = lax.axis_size("view"), lax.axis_size("head")
+    view, group = lax.axis_index("view"), lax.axis_index("head")
+    features = out_weight.shape[0]
+    share, columns = features // views, out_weight.shape[1] // groups
+    mine = lax.dynamic_slice_in_dim(out_weight, view * share, share, 0)
+    rows = jnp.zeros((groups, share, columns), out_weight.dtype)
+    for step in range(groups):
+        to, source = (group + step) % groups, (group - step) % groups
+        block = lax.dynamic_slice_in_dim(mine, to * columns, columns, 1)
+        block = block if step == 0 else shift(block, "head", step)
+        rows = lax.dynamic_update_index_in_dim(rows, block, source, 0)
+    rows, _ = lax.optimization_barrier((rows, after))
+    full = jnp.zeros((groups, features, columns), out_weight.dtype)
+    for step in range(views):
+        source = (view - step) % views
+        block = rows if step == 0 else shift(rows, "view", step)
+        full = lax.dynamic_update_slice_in_dim(full, block, source * share, 1)
+    return full
+
+
 def local(query, key, value, out_weight, pairs, counts):
     views = lax.axis_size("view")
     groups = lax.axis_size("head")
     me = lax.axis_index("view")
     features = query.shape[1]
     heads = features // HEAD_DIM
-    chunks = 3 if heads % 3 == 0 else 1
+    chunks = heads
     per = heads // chunks
     width = per * HEAD_DIM
 
@@ -141,19 +167,14 @@
         )
         for c in range(chunks)
     ]
-    share = features // views
-    mine = lax.dynamic_slice_in_dim(out_weight, me * share, share, 0)
-    mine = lax.all_to_all(
-        mine.reshape(share, groups, -1), "head", split_axis=1, concat_axis=1, tiled=True
-    )
-    weight = lax.all_gather(mine, "view", axis=0, tiled=True)
+    weight = spread_weight(out_weight, incoming[min(1, chunks - 1)])
 
     total = None
     for c in range(chunks):
         attended = attend(meta, query, key, value, incoming[c], c, per)
         gathered = lax.all_gather(attended, "head", axis=0, tiled=False)
         gathered = gathered.reshape(groups * width, -1)
-        part = jnp.swapaxes(weight[c * width : (c + 1) * width], 0, 1)
+        part = weight[:, c * width : (c + 1) * width]
         term = lax.dot_general(
             part.reshape(groups * width, -1),
             gathered,

time: 317 us -> 412 us (1.30)
  local copies, waits for them, and re-layouts: 27.6 us -> 131 us
  waiting for transfers between devices: 101 us -> 58.3 us
  matrix products: 21.8 us -> 37.7 us
  starting transfers between devices: 4.58 us -> 20.3 us
  Pallas kernels: 42 us -> 54.2 us
  blocking collectives: 104 us -> 94.2 us
    dynamic_update_slice x0 -> x12, local copies, waits for them, and re-layouts: none -> 90.2 us  [the longest x8 88.2 us: spread_weight(): full = lax.dynamic_update_slice_in_dim(full, block, source * share, 1)]
    all_gather x3 -> x6, waiting for transfers between devices: 49.4 us -> 0.01 us  [local(): gathered = lax.all_gather(attended, 'head', axis=0, tiled=False)]
    ppermute x0 -> x10, waiting for transfers between devices: none -> 37.8 us  [shift(): lax.ppermute(array, axis, [(i, (i + step) % size) for i in range(size)])]
    all_to_all x1 -> x2, waiting for transfers between devices: 51.9 us -> 20.4 us  [local(): lax.all_to_all(collect(source_tiles, key, value, c, width), 'view', 0, 0,...]
    all_to_all x1 -> x0, blocking collectives: 22 us -> none  [local(): lax.all_to_all(mine.reshape(share, groups, -1), 'head', split_axis=1, con...]
    dot_general x3 -> x6, matrix products: 21.8 us -> 37.7 us  [local(): lax.dot_general(part.reshape(groups * width, -1), gathered, (((0,), (0,))...]
    all_to_all x2 -> x4, blocking collectives: 81.9 us -> 94.2 us  [local(): lax.all_to_all(collect(source_tiles, key, value, c, width), 'view', 0, 0,...]
    ppermute x0 -> x10, starting transfers between devices: none -> 10.5 us  [shift(): lax.ppermute(array, axis, [(i, (i + step) % size) for i in range(size)])]
  transfers between devices with their start and end apart: 5 -> 18, of which waited for: 2 -> 4; matrix products, arithmetic and copies ran while one was open for 10% -> 33% of each run, Pallas kernels for 13% -> 11%
where the time goes in v2:
time: 412 us; the launch traced here: 411 us
  local copies, waits for them, and re-layouts  131 us (32%)
  blocking collectives  94.2 us (23%)
  waiting for transfers between devices  58.3 us (14%)
  Pallas kernels  54.2 us (13%)
  matrix products  37.7 us (9%)
  starting transfers between devices  20.3 us (5%)
  between operations  14.1 us (3%)
    all_to_all x4, blocking collectives, local(): lax.all_to_all(collect(source_tiles, key, value, c, width), 'view', 0, 0,...  94.2 us
    dynamic_update_slice x8, local copies, waits for them, and re-layouts, spread_weight(): full = lax.dynamic_update_slice_in_dim(full, block, source * share, 1)  88.2 us
    pallas_call x6, Pallas kernels, attend(): pl.pallas_call(functools.partial(attend_kernel, slots, tile), grid_spec=p...  46.7 us
    ppermute x10, waiting for transfers between devices, shift(): lax.ppermute(array, axis, [(i, (i + step) % size) for i in range(size)])  37.8 us
    dot_general x6, matrix products, local(): lax.dot_general(part.reshape(groups * width, -1), gathered, (((0,), (0,))...  37.7 us
    unnamed x47, local copies, waits for them, and re-layouts  23.1 us
    all_to_all x2, waiting for transfers between devices, local(): lax.all_to_all(collect(source_tiles, key, value, c, width), 'view', 0, 0,...  20.4 us
    ppermute x10, starting transfers between devices, shift(): lax.ppermute(array, axis, [(i, (i + step) % size) for i in range(size)])  10.5 us
  transfers between devices with their start and end apart: 18, of which 4 were waited for; matrix products, arithmetic and copies ran while one was open for 33% of the time, Pallas kernels for 11%

profile of v2, /device:TPU:0, one launch (start us, length us, event | category | flops | bytes accessed | tf_op | source)
XLA Modules:
  0.0 410.9 jit_solution(780249325947826694)
XLA Ops:
  9.3 1.7 copy-done
  11.0 1.7 copy-done.2
  15.0 5.2 %all-to-all-start.4 = ((bf16[8,384,256]{2,1,0:T(8,128)(2,1)}), bf16[8,384,256]{2,1,0:T(8,128)(2,1)}, u32[]{:S(2)}, u32[]{:S(2)}) async-start(bf16[8,384,256]{2,1,0:T(8,128)(2,1)} %copy-done.21), calls=%async_computation.4 | async-start | bytes 3145728 | tf_op jit(solution)/shard_map/all_to_all | solution.py:165
  21.0 20.4 %all-to-all-done.4.pk_ref.pv_ref = bf16[8,384,256]{2,1,0:T(8,128)(2,1)} async-done(((bf16[8,384,256]{2,1,0:T(8,128)(2,1)}), bf16[8,384,256]{2,1,0:T(8,128)(2,1)}, u32[]{:S(2)}, u32[]{:S(2)}) %all-to-all-start.4) | async-done | bytes 1572896 | tf_op jit(solution)/shard_map/all_to_all | solution.py:165
  41.4 1.7 copy-done.3
  43.1 1.7 copy-done.14
  44.8 8.6 %shard_map.73 = bf16[128,1536]{1,0:T(8,128)(2,1)} custom-call(s32[15]{0:T(128)S(1)} %pad_add_fusion.meta_ref, bf16[1536,768]{1,0:T(8,128)(2,1)S(1)} %copy-done.14, bf16[1536,768]{1,0:T(8,128)(2,1)S(1)} %copy-done.1, bf16[1536,768]{1,0:T(8,128)(2,1)S(1)} %copy-done.3, bf16[8,384,256]{2,1,0:T(8,128)(2,1)} %all-to-all-done.4.pk_ref.pv_ref, ...), custom_call_target="tpu_custom_call" | custom-call | flops 1660944384 | bytes 3145728 | tf_op jit(solution)/shard_map/pallas_call | solution.py:97
  53.4 1.7 copy-done.4
  56.3 23.5 %all_to_all.30.pk_ref.pv_ref = bf16[8,384,256]{2,1,0:T(8,128)(2,1)S(1)} all-to-all(bf16[8,384,256]{2,1,0:T(8,128)(2,1)S(1)} %shard_map.70), channel_id=1, replica_groups=mesh['view'=8,'head'=4] {'view'}, dimensions={0} | all-to-all | bytes 3145728 | tf_op jit(solution)/shard_map/all_to_all | solution.py:165
  79.9 7.3 %shard_map.71 = bf16[128,1536]{1,0:T(8,128)(2,1)} custom-call(s32[15]{0:T(128)S(1)} %pad_add_fusion.meta_ref, bf16[1536,768]{1,0:T(8,128)(2,1)S(1)} %copy-done.15, bf16[1536,768]{1,0:T(8,128)(2,1)S(1)} %copy-done.1, bf16[1536,768]{1,0:T(8,128)(2,1)S(1)} %copy-done.5, bf16[8,384,256]{2,1,0:T(8,128)(2,1)S(1)} %all_to_all.30.pk_ref.pv_ref, ...), custom_call_target="tpu_custom_call" | custom-call | flops 1660944384 | bytes 3145728 | tf_op jit(solution)/shard_map/pallas_call | solution.py:97
  87.3 1.7 copy-done.6
  90.2 23.5 %all_to_all.31.pk_ref.pv_ref = bf16[8,384,256]{2,1,0:T(8,128)(2,1)S(1)} all-to-all(bf16[8,384,256]{2,1,0:T(8,128)(2,1)S(1)} %shard_map.68), channel_id=1, replica_groups=mesh['view'=8,'head'=4] {'view'}, dimensions={0} | all-to-all | bytes 3145728 | tf_op jit(solution)/shard_map/all_to_all | solution.py:165
  113.8 7.4 %shard_map.69 = bf16[128,1536]{1,0:T(8,128)(2,1)} custom-call(s32[15]{0:T(128)S(1)} %pad_add_fusion.meta_ref, bf16[1536,768]{1,0:T(8,128)(2,1)S(1)} %copy-done.16, bf16[1536,768]{1,0:T(8,128)(2,1)S(1)} %copy-done.1, bf16[1536,768]{1,0:T(8,128)(2,1)S(1)} %copy-done.7, bf16[8,384,256]{2,1,0:T(8,128)(2,1)S(1)} %all_to_all.31.pk_ref.pv_ref, ...), custom_call_target="tpu_custom_call" | custom-call | flops 1660944384 | bytes 3145728 | tf_op jit(solution)/shard_map/pallas_call | solution.py:97
  121.2 1.7 copy-done.8
  124.1 23.5 %all_to_all.32.pk_ref.pv_ref = bf16[8,384,256]{2,1,0:T(8,128)(2,1)S(1)} all-to-all(bf16[8,384,256]{2,1,0:T(8,128)(2,1)S(1)} %shard_map.64), channel_id=1, replica_groups=mesh['view'=8,'head'=4] {'view'}, dimensions={0} | all-to-all | bytes 3145728 | tf_op jit(solution)/shard_map/all_to_all | solution.py:165
  147.7 7.3 %shard_map.67 = bf16[128,1536]{1,0:T(8,128)(2,1)} custom-call(s32[15]{0:T(128)S(1)} %pad_add_fusion.meta_ref, bf16[1536,768]{1,0:T(8,128)(2,1)S(1)} %copy-done.17, bf16[1536,768]{1,0:T(8,128)(2,1)S(1)} %copy-done.1, bf16[1536,768]{1,0:T(8,128)(2,1)S(1)} %copy-done.9, bf16[8,384,256]{2,1,0:T(8,128)(2,1)S(1)} %all_to_all.32.pk_ref.pv_ref, ...), custom_call_target="tpu_custom_call" | custom-call | flops 1660944384 | bytes 3145728 | tf_op jit(solution)/shard_map/pallas_call | solution.py:97
  155.1 1.7 copy-done.10
  158.0 23.5 %all_to_all.33.pk_ref.pv_ref = bf16[8,384,256]{2,1,0:T(8,128)(2,1)S(1)} all-to-all(bf16[8,384,256]{2,1,0:T(8,128)(2,1)S(1)} %shard_map.65), channel_id=1, replica_groups=mesh['view'=8,'head'=4] {'view'}, dimensions={0} | all-to-all | bytes 3145728 | tf_op jit(solution)/shard_map/all_to_all | solution.py:165
  181.6 7.5 %shard_map.66 = bf16[128,1536]{1,0:T(8,128)(2,1)} custom-call(s32[15]{0:T(128)S(1)} %pad_add_fusion.meta_ref, bf16[1536,768]{1,0:T(8,128)(2,1)S(1)} %copy-done.18, bf16[1536,768]{1,0:T(8,128)(2,1)S(1)} %copy-done.1, bf16[1536,768]{1,0:T(8,128)(2,1)S(1)} %copy-done.11, bf16[8,384,256]{2,1,0:T(8,128)(2,1)S(1)} %all_to_all.33.pk_ref.pv_ref, ...), custom_call_target="tpu_custom_call" | custom-call | flops 1660944384 | bytes 3145728 | tf_op jit(solution)/shard_map/pallas_call | solution.py:97
  189.2 1.6 fusion.13
  191.6 2.0 collective-permute-start
  194.4 2.6 collective-permute-start.1
  199.1 1.7 copy-done.12
  203.2 4.3 %all-to-all-start.5 = ((bf16[8,384,256]{2,1,0:T(8,128)(2,1)}), bf16[8,384,256]{2,1,0:T(8,128)(2,1)}, u32[]{:S(2)}, u32[]{:S(2)}) async-start(bf16[8,384,256]{2,1,0:T(8,128)(2,1)} %copy-done.20), calls=%async_computation.5 | async-start | bytes 3145728 | tf_op jit(solution)/shard_map/all_to_all | solution.py:165
  208.9 6.9 %collective-permute-done.1 = bf16[96,768]{0,1:T(8,128)(2,1)} collective-permute-done((bf16[96,768]{0,1:T(8,128)(2,1)}, bf16[96,768]{0,1:T(8,128)(2,1)}, u32[]{:S(2)}, u32[]{:S(2)}) %collective-permute-start.1) | collective-permute-done | bytes 147488 | tf_op jit(solution)/shard_map/ppermute | solution.py:122
  218.9 2.4 collective-permute-start.5
  222.1 19.6 %collective-permute-done.4 = bf16[4,96,768]{2,1,0:T(8,128)(2,1)} collective-permute-done((bf16[4,96,768]{2,1,0:T(8,128)(2,1)}, bf16[4,96,768]{2,1,0:T(8,128)(2,1)}, u32[]{:S(2)}, u32[]{:S(2)}) %collective-permute-start.4) | collective-permute-done | bytes 589856 | tf_op jit(solution)/shard_map/ppermute | solution.py:122
  242.2 11.2 %collective-permute-done.3 = bf16[4,96,768]{2,1,0:T(8,128)(2,1)} collective-permute-done((bf16[4,96,768]{2,1,0:T(8,128)(2,1)}, bf16[4,96,768]{2,1,0:T(8,128)(2,1)}, u32[]{:S(2)}, u32[]{:S(2)}) %collective-permute-start.3) | collective-permute-done | bytes 589856 | tf_op jit(solution)/shard_map/ppermute | solution.py:122
  253.4 1.7 copy-done.13
  255.1 1.7 copy-done.19
  256.8 8.6 %shard_map.75 = bf16[128,1536]{1,0:T(8,128)(2,1)} custom-call(s32[15]{0:T(128)S(1)} %pad_add_fusion.meta_ref, bf16[1536,768]{1,0:T(8,128)(2,1)S(1)} %copy-done.19, bf16[1536,768]{1,0:T(8,128)(2,1)S(1)} %copy-done.1, bf16[1536,768]{1,0:T(8,128)(2,1)S(1)} %copy-done.13, bf16[8,384,256]{2,1,0:T(8,128)(2,1)} %all-to-all-done.5.pk_ref.pv_ref, ...), custom_call_target="tpu_custom_call" | custom-call | flops 1660944384 | bytes 3145728 | tf_op jit(solution)/shard_map/pallas_call | solution.py:97
  265.5 2.5 broadcast_in_dim.35
  268.0 10.0 %dynamic_update_slice.41 = bf16[4,768,768]{1,2,0:T(8,128)(2,1)} dynamic-update-slice(bf16[4,768,768]{1,2,0:T(8,128)(2,1)} %broadcast_in_dim.35, bf16[4,96,768]{1,2,0:T(8,128)(2,1)S(1)} %bitcast_dynamic-update-slice_fusion, s32[]{:T(128)} %constant.155.clone.1, s32[]{:T(128)S(6)} %select_n.159, s32[]{:T(128)} %constant.155.clone.1) | dynamic-update-slice | bytes 1179652 | tf_op jit(solution)/shard_map/dynamic_update_slice | solution.py:142
  279.5 10.8 %dynamic_update_slice.42 = bf16[4,768,768]{1,2,0:T(8,128)(2,1)} dynamic-update-slice(bf16[4,768,768]{1,2,0:T(8,128)(2,1)} %dynamic_update_slice.41, bf16[4,96,768]{1,2,0:T(8,128)(2,1)S(1)} %copy.34, s32[]{:T(128)} %constant.155.clone.1, s32[]{:T(128)S(6)} %select_n.161, s32[]{:T(128)} %constant.155.clone.1) | dynamic-update-slice | bytes 1179652 | tf_op jit(solution)/shard_map/dynamic_update_slice | solution.py:142
  291.7 11.5 %dynamic_update_slice.43 = bf16[4,768,768]{1,2,0:T(8,128)(2,1)} dynamic-update-slice(bf16[4,768,768]{1,2,0:T(8,128)(2,1)} %dynamic_update_slice.42, bf16[4,96,768]{1,2,0:T(8,128)(2,1)S(1)} %copy.36, s32[]{:T(128)} %constant.155.clone.1, s32[]{:T(128)S(6)} %select_n.163, s32[]{:T(128)} %constant.155.clone.1) | dynamic-update-slice | bytes 1179652 | tf_op jit(solution)/shard_map/dynamic_update_slice | solution.py:142
  304.6 11.4 %dynamic_update_slice.44 = bf16[4,768,768]{1,2,0:T(8,128)(2,1)} dynamic-update-slice(bf16[4,768,768]{1,2,0:T(8,128)(2,1)} %dynamic_update_slice.43, bf16[4,96,768]{1,2,0:T(8,128)(2,1)S(1)} %copy.38, s32[]{:T(128)} %constant.155.clone.1, s32[]{:T(128)S(6)} %select_n.165, s32[]{:T(128)} %constant.155.clone.1) | dynamic-update-slice | bytes 1179652 | tf_op jit(solution)/shard_map/dynamic_update_slice | solution.py:142
  316.0 1.4 copy.40
  317.5 10.0 %dynamic_update_slice.45 = bf16[4,768,768]{1,2,0:T(8,128)(2,1)} dynamic-update-slice(bf16[4,768,768]{1,2,0:T(8,128)(2,1)} %dynamic_update_slice.44, bf16[4,96,768]{1,2,0:T(8,128)(2,1)S(1)} %copy.40, s32[]{:T(128)} %constant.155.clone.1, s32[]{:T(128)S(6)} %select_n.167, s32[]{:T(128)} %constant.155.clone.1) | dynamic-update-slice | bytes 1179652 | tf_op jit(solution)/shard_map/dynamic_update_slice | solution.py:142
  327.5 1.4 copy.42
  328.9 11.5 %dynamic_update_slice.46 = bf16[4,768,768]{1,2,0:T(8,128)(2,1)} dynamic-update-slice(bf16[4,768,768]{1,2,0:T(8,128)(2,1)} %dynamic_update_slice.45, bf16[4,96,768]{1,2,0:T(8,128)(2,1)S(1)} %copy.42, s32[]{:T(128)} %constant.155.clone.1, s32[]{:T(128)S(6)} %select_n.169, s32[]{:T(128)} %constant.155.clone.1) | dynamic-update-slice | bytes 1179652 | tf_op jit(solution)/shard_map/dynamic_update_slice | solution.py:142
  341.9 11.5 %dynamic_update_slice.47 = bf16[4,768,768]{1,2,0:T(8,128)(2,1)} dynamic-update-slice(bf16[4,768,768]{1,2,0:T(8,128)(2,1)} %dynamic_update_slice.46, bf16[4,96,768]{1,2,0:T(8,128)(2,1)S(1)} %copy.44, s32[]{:T(128)} %constant.155.clone.1, s32[]{:T(128)S(6)} %select_n.171, s32[]{:T(128)} %constant.155.clone.1) | dynamic-update-slice | bytes 1179652 | tf_op jit(solution)/shard_map/dynamic_update_slice | solution.py:142
  354.8 11.5 %dynamic_update_slice.48 = bf16[4,768,768]{1,2,0:T(8,128)(2,1)} dynamic-update-slice(bf16[4,768,768]{1,2,0:T(8,128)(2,1)} %dynamic_update_slice.47, bf16[4,96,768]{1,2,0:T(8,128)(2,1)S(1)} %copy.46, s32[]{:T(128)} %constant.155.clone.1, s32[]{:T(128)S(6)} %select_n.173, s32[]{:T(128)} %constant.155.clone.1) | dynamic-update-slice | bytes 1179652 | tf_op jit(solution)/shard_map/dynamic_update_slice | solution.py:142
  366.3 5.2 %fusion.2 = f32[768,1536,1]{1,0,2:T(8,128)} fusion(bf16[4,128,1536]{2,1,0:T(8,128)(2,1)} %bitcast.50, bf16[4,768,768]{1,2,0:T(8,128)(2,1)} %dynamic_update_slice.48), kind=kOutput, calls=%fused_computation.7 | convolution fusion | flops 1207959552 | bytes 7077888 | tf_op jit(solution)/shard_map/dot_general | solution.py:178
  371.5 5.2 %fusion.4 = f32[768,1536,1]{1,0,2:T(8,128)} fusion(bf16[4,128,1536]{2,1,0:T(8,128)(2,1)} %bitcast.51, bf16[4,768,768]{1,2,0:T(8,128)(2,1)} %dynamic_update_slice.48), kind=kOutput, calls=%fused_computation.9 | convolution fusion | flops 1207959552 | bytes 7077888 | tf_op jit(solution)/shard_map/dot_general | solution.py:178
  376.8 5.3 %fusion.6 = f32[768,1536,1]{1,0,2:T(8,128)} fusion(bf16[4,128,1536]{2,1,0:T(8,128)(2,1)} %bitcast.52, bf16[4,768,768]{1,2,0:T(8,128)(2,1)} %dynamic_update_slice.48), kind=kOutput, calls=%fused_computation.11 | convolution fusion | flops 1207959552 | bytes 7077888 | tf_op jit(solution)/shard_map/dot_general | solution.py:178
  382.1 5.2 %fusion.8 = f32[768,1536,1]{1,0,2:T(8,128)} fusion(bf16[4,128,1536]{2,1,0:T(8,128)(2,1)} %bitcast.53, bf16[4,768,768]{1,2,0:T(8,128)(2,1)} %dynamic_update_slice.48), kind=kOutput, calls=%fused_computation.13 | convolution fusion | flops 1207959552 | bytes 7077888 | tf_op jit(solution)/shard_map/dot_general | solution.py:178
  387.3 5.2 %fusion.10 = f32[768,1536,1]{1,0,2:T(8,128)} fusion(bf16[4,128,1536]{2,1,0:T(8,128)(2,1)} %bitcast.54, bf16[4,768,768]{1,2,0:T(8,128)(2,1)} %dynamic_update_slice.48), kind=kOutput, calls=%fused_computation.15 | convolution fusion | flops 1207959552 | bytes 7077888 | tf_op jit(solution)/shard_map/dot_general | solution.py:178
  392.5 11.5 %fusion = bf16[768,1536]{1,0:T(8,128)(2,1)} fusion(f32[768,1536,1]{1,0,2:T(8,128)} %fusion.2, f32[768,1536,1]{1,0,2:T(8,128)} %fusion.4, f32[768,1536,1]{1,0,2:T(8,128)} %fusion.6, f32[768,1536,1]{1,0,2:T(8,128)} %fusion.8, f32[768,1536,1]{1,0,2:T(8,128)} %fusion.10, bf16[4,128,1536]{2,1,0:T(8,128)(2,1)} %bitcast.48, ...), kind=kOutput, calls=%fused_computation.1 | convolution fusion | flops 1215037440 | bytes 28311552 | tf_op jit(solution)/shard_map/dot_general | solution.py:178
  (92 shorter events, 30.2 us)
Async XLA Ops:
  9.3 1.7 copy-start
  11.0 1.7 copy-start.2
  12.7 28.8 %copy-start.1 = (bf16[1536,768]{1,0:T(8,128)(2,1)S(1)}, bf16[1536,768]{1,0:T(8,128)(2,1)}, u32[]{:S(2)}) copy-start(bf16[1536,768]{1,0:T(8,128)(2,1)} %k_ref.11) | copy-start | bytes 7077892
  13.9 1.1 copy-start.21
  15.0 26.4 %all-to-all-start.4 = ((bf16[8,384,256]{2,1,0:T(8,128)(2,1)}), bf16[8,384,256]{2,1,0:T(8,128)(2,1)}, u32[]{:S(2)}, u32[]{:S(2)}) async-start(bf16[8,384,256]{2,1,0:T(8,128)(2,1)} %copy-done.21), calls=%async_computation.4 | async-start | bytes 3145728 | tf_op jit(solution)/shard_map/all_to_all | solution.py:165
  20.3 346.0 %all-gather.21.cloned.1.call-start = ((), (), s32[]{:S(2)}) async-start(), calls=%async_computation.10 | async-start | bytes 1966080 | tf_op jit(solution)/shard_map/all_gather | solution.py:175
  41.4 1.7 copy-start.3
  43.1 1.7 copy-start.14
  53.4 318.2 %all-gather.19.cloned.1.call-start = ((), (), s32[]{:S(2)}) async-start(), calls=%async_computation.9 | async-start | bytes 1966080 | tf_op jit(solution)/shard_map/all_gather | solution.py:175
  53.4 1.7 copy-start.4
  55.1 24.8 %copy-start.5 = (bf16[1536,768]{1,0:T(8,128)(2,1)S(1)}, bf16[1536,768]{1,0:T(8,128)(2,1)}, u32[]{:S(2)}) copy-start(bf16[1536,768]{1,0:T(8,128)(2,1)} %v_ref.11) | copy-start | bytes 7077892
  55.1 24.8 %copy-start.15 = (bf16[1536,768]{1,0:T(8,128)(2,1)S(1)}, bf16[1536,768]{1,0:T(8,128)(2,1)}, u32[]{:S(2)}) copy-start(bf16[1536,768]{1,0:T(8,128)(2,1)} %q_ref.11) | copy-start | bytes 7077892
  87.2 289.5 %all-gather.17.cloned.1.call-start = ((), (), s32[]{:S(2)}) async-start(), calls=%async_computation.8 | async-start | bytes 1966080 | tf_op jit(solution)/shard_map/all_gather | solution.py:175
  87.3 1.7 copy-start.6
  89.0 24.8 %copy-start.7 = (bf16[1536,768]{1,0:T(8,128)(2,1)S(1)}, bf16[1536,768]{1,0:T(8,128)(2,1)}, u32[]{:S(2)}) copy-start(bf16[1536,768]{1,0:T(8,128)(2,1)} %v_ref.11) | copy-start | bytes 7077892
  89.0 24.8 %copy-start.16 = (bf16[1536,768]{1,0:T(8,128)(2,1)S(1)}, bf16[1536,768]{1,0:T(8,128)(2,1)}, u32[]{:S(2)}) copy-start(bf16[1536,768]{1,0:T(8,128)(2,1)} %q_ref.11) | copy-start | bytes 7077892
  121.1 260.9 %all-gather.15.cloned.1.call-start = ((), (), s32[]{:S(2)}) async-start(), calls=%async_computation.7 | async-start | bytes 1966080 | tf_op jit(solution)/shard_map/all_gather | solution.py:175
  121.2 1.7 copy-start.8
  122.9 24.8 %copy-start.9 = (bf16[1536,768]{1,0:T(8,128)(2,1)S(1)}, bf16[1536,768]{1,0:T(8,128)(2,1)}, u32[]{:S(2)}) copy-start(bf16[1536,768]{1,0:T(8,128)(2,1)} %v_ref.11) | copy-start | bytes 7077892
  122.9 24.8 %copy-start.17 = (bf16[1536,768]{1,0:T(8,128)(2,1)S(1)}, bf16[1536,768]{1,0:T(8,128)(2,1)}, u32[]{:S(2)}) copy-start(bf16[1536,768]{1,0:T(8,128)(2,1)} %q_ref.11) | copy-start | bytes 7077892
  155.0 232.2 %all-gather.13.cloned.1.call-start = ((), (), s32[]{:S(2)}) async-start(), calls=%async_computation.6 | async-start | bytes 1966080 | tf_op jit(solution)/shard_map/all_gather | solution.py:175
  155.1 1.7 copy-start.10
  156.8 24.8 %copy-start.11 = (bf16[1536,768]{1,0:T(8,128)(2,1)S(1)}, bf16[1536,768]{1,0:T(8,128)(2,1)}, u32[]{:S(2)}) copy-start(bf16[1536,768]{1,0:T(8,128)(2,1)} %v_ref.11) | copy-start | bytes 7077892
  156.8 24.8 %copy-start.18 = (bf16[1536,768]{1,0:T(8,128)(2,1)S(1)}, bf16[1536,768]{1,0:T(8,128)(2,1)}, u32[]{:S(2)}) copy-start(bf16[1536,768]{1,0:T(8,128)(2,1)} %q_ref.11) | copy-start | bytes 7077892
  191.6 16.4 %collective-permute-start = (bf16[96,768]{0,1:T(8,128)(2,1)}, bf16[96,768]{0,1:T(8,128)(2,1)}, u32[]{:S(2)}, u32[]{:S(2)}) collective-permute-start(bf16[96,768]{0,1:T(8,128)(2,1)} %copy.47), channel_id=1, source_target_pairs={{0,1},{1,2},{2,3},{3,0},{4,5},{5,6},{6,7},{7,4},{8,9},{9,10},{10,1... | collective-permute-start | bytes 442376 | tf_op jit(solution)/shard_map/ppermute | solution.py:122
  194.4 21.5 %collective-permute-start.1 = (bf16[96,768]{0,1:T(8,128)(2,1)}, bf16[96,768]{0,1:T(8,128)(2,1)}, u32[]{:S(2)}, u32[]{:S(2)}) collective-permute-start(bf16[96,768]{0,1:T(8,128)(2,1)} %copy.48), channel_id=1, source_target_pairs={{0,2},{1,3},{2,0},{3,1},{4,6},{5,7},{6,4},{7,5},{8,10},{9,11},{10,... | collective-permute-start | bytes 442376 | tf_op jit(solution)/shard_map/ppermute | solution.py:122
  197.8 19.1 %collective-permute-start.2 = (bf16[96,768]{0,1:T(8,128)(2,1)}, bf16[96,768]{0,1:T(8,128)(2,1)S(1)}, u32[]{:S(2)}, u32[]{:S(2)}) collective-permute-start(bf16[96,768]{0,1:T(8,128)(2,1)} %copy.49), channel_id=1, source_target_pairs={{0,3},{1,0},{2,1},{3,2},{4,7},{5,4},{6,5},{7,6},{8,11},{9,8},{10,9... | collective-permute-start | bytes 442376 | tf_op jit(solution)/shard_map/ppermute | solution.py:122
  199.1 1.7 copy-start.12
  202.0 1.1 copy-start.20
  203.2 50.2 %all-to-all-start.5 = ((bf16[8,384,256]{2,1,0:T(8,128)(2,1)}), bf16[8,384,256]{2,1,0:T(8,128)(2,1)}, u32[]{:S(2)}, u32[]{:S(2)}) async-start(bf16[8,384,256]{2,1,0:T(8,128)(2,1)} %copy-done.20), calls=%async_computation.5 | async-start | bytes 3145728 | tf_op jit(solution)/shard_map/all_to_all | solution.py:165
  207.5 185.0 %all-gather.23.cloned.1.call-start = ((), (), s32[]{:S(2)}) async-start(), calls=%async_computation.11 | async-start | bytes 1966080 | tf_op jit(solution)/shard_map/all_gather | solution.py:175
  218.0 23.8 %collective-permute-start.4 = (bf16[4,96,768]{2,1,0:T(8,128)(2,1)}, bf16[4,96,768]{2,1,0:T(8,128)(2,1)}, u32[]{:S(2)}, u32[]{:S(2)}) collective-permute-start(bf16[4,96,768]{2,1,0:T(8,128)(2,1)} %copy.33), channel_id=1, source_target_pairs={{0,8},{4,12},{8,16},{12,20},{16,24},{20,28},{24,0},{28,4},{1,9},{5... | collective-permute-start | bytes 1769480 | tf_op jit(solution)/shard_map/ppermute | solution.py:122
  218.9 34.5 %collective-permute-start.3 = (bf16[4,96,768]{2,1,0:T(8,128)(2,1)}, bf16[4,96,768]{2,1,0:T(8,128)(2,1)}, u32[]{:S(2)}, u32[]{:S(2)}) collective-permute-start(bf16[4,96,768]{2,1,0:T(8,128)(2,1)} %copy.33), channel_id=1, source_target_pairs={{0,4},{4,8},{8,12},{12,16},{16,20},{20,24},{24,28},{28,0},{1,5},{5... | collective-permute-start | bytes 1769480 | tf_op jit(solution)/shard_map/ppermute | solution.py:122
  218.9 84.2 %collective-permute-start.5 = (bf16[4,96,768]{2,1,0:T(8,128)(2,1)}, bf16[4,96,768]{2,1,0:T(8,128)(2,1)}, u32[]{:S(2)}, u32[]{:S(2)}) collective-permute-start(bf16[4,96,768]{2,1,0:T(8,128)(2,1)} %copy.33), channel_id=1, source_target_pairs={{0,12},{4,16},{8,20},{12,24},{16,28},{20,0},{24,4},{28,8},{1,13},{... | collective-permute-start | bytes 1769480 | tf_op jit(solution)/shard_map/ppermute | solution.py:122
  221.3 94.7 %collective-permute-start.6 = (bf16[4,96,768]{2,1,0:T(8,128)(2,1)}, bf16[4,96,768]{2,1,0:T(8,128)(2,1)}, u32[]{:S(2)}, u32[]{:S(2)}) collective-permute-start(bf16[4,96,768]{2,1,0:T(8,128)(2,1)} %copy.33), channel_id=1, source_target_pairs={{0,16},{4,20},{8,24},{12,28},{16,0},{20,4},{24,8},{28,12},{1,17},{... | collective-permute-start | bytes 1769480 | tf_op jit(solution)/shard_map/ppermute | solution.py:122
  222.1 105.4 %collective-permute-start.7 = (bf16[4,96,768]{2,1,0:T(8,128)(2,1)}, bf16[4,96,768]{2,1,0:T(8,128)(2,1)}, u32[]{:S(2)}, u32[]{:S(2)}) collective-permute-start(bf16[4,96,768]{2,1,0:T(8,128)(2,1)} %copy.33), channel_id=1, source_target_pairs={{0,20},{4,24},{8,28},{12,0},{16,4},{20,8},{24,12},{28,16},{1,21},{... | collective-permute-start | bytes 1769480 | tf_op jit(solution)/shard_map/ppermute | solution.py:122
  241.7 98.7 %collective-permute-start.8 = (bf16[4,96,768]{2,1,0:T(8,128)(2,1)}, bf16[4,96,768]{2,1,0:T(8,128)(2,1)}, u32[]{:S(2)}, u32[]{:S(2)}) collective-permute-start(bf16[4,96,768]{2,1,0:T(8,128)(2,1)} %copy.33), channel_id=1, source_target_pairs={{0,24},{4,28},{8,0},{12,4},{16,8},{20,12},{24,16},{28,20},{1,25},{... | collective-permute-start | bytes 1769480 | tf_op jit(solution)/shard_map/ppermute | solution.py:122
  253.4 100.0 %collective-permute-start.9 = (bf16[4,96,768]{2,1,0:T(8,128)(2,1)}, bf16[4,96,768]{2,1,0:T(8,128)(2,1)}, u32[]{:S(2)}, u32[]{:S(2)}) collective-permute-start(bf16[4,96,768]{2,1,0:T(8,128)(2,1)} %copy.33), channel_id=1, source_target_pairs={{0,28},{4,0},{8,4},{12,8},{16,12},{20,16},{24,20},{28,24},{1,29},{... | collective-permute-start | bytes 1769480 | tf_op jit(solution)/shard_map/ppermute | solution.py:122
  253.4 1.7 copy-start.13
  255.1 1.7 copy-start.19
Sparse Core Ops, SparseCore 0:
  53.5 36.8 all-gather.20
  91.9 35.9 all-gather.18
  129.5 35.9 all-gather.16
  166.9 48.4 all-gather.14
  216.8 36.6 all-gather.12
  265.5 33.5 all-gather.22

commit v3 on v1

--- a/solution.py
+++ b/solution.py
@@ -90,7 +90,7 @@
     tile = tokens // TILES
     views = incoming.shape[0]
     slots = (meta.shape[0] - 1) // 2
-    own = pl.BlockSpec((tokens, HEAD_DIM), lambda h, meta: (0, chunk * heads + h))
+    own = pl.BlockSpec((tokens, HEAD_DIM), lambda h, meta: (0, chunk + h))
     peer_key = pl.BlockSpec((views, tile, HEAD_DIM), lambda h, meta: (0, 0, h))
     peer_value = pl.BlockSpec((views, tile, HEAD_DIM), lambda h, meta: (0, 0, heads + h))
     blocks = heads * (TILES + min(slots, 7)) * tile * tile
@@ -117,15 +117,68 @@
     )(meta, query, key, value, incoming, incoming)
 
 
+def shift(array, axis, step):
+    size = lax.axis_size(axis)
+    return lax.ppermute(array, axis, [(i, (i + step) % size) for i in range(size)])
+
+
+def weight_rows(out_weight):
+    groups = lax.axis_size("head")
+    view, group = lax.axis_index("view"), lax.axis_index("head")
+    share = out_weight.shape[0] // lax.axis_size("view")
+    columns = out_weight.shape[1] // groups
+    mine = lax.dynamic_slice_in_dim(out_weight, view * share, share, 0)
+    blocks = []
+    for step in range(groups):
+        block = lax.dynamic_slice_in_dim(
+            mine, lax.rem(group + step, groups) * columns, columns, 1
+        )
+        blocks.append(block if step == 0 else shift(block, "head", step))
+    return jnp.stack(blocks)
+
+
+def order_kernel(at_ref, in_ref, out_ref):
+    out_ref[...] = in_ref[...]
+
+
+def spread_weight(rows):
+    views, groups = lax.axis_size("view"), lax.axis_size("head")
+    _, share, columns = rows.shape
+    stack = jnp.stack([rows] + [shift(rows, "view", step) for step in range(1, views)])
+    at = jnp.stack([lax.axis_index("view"), lax.axis_index("head")])
+    block = (1, 1, share, columns)
+    ordered = pl.pallas_call(
+        order_kernel,
+        grid_spec=pltpu.PrefetchScalarGridSpec(
+            num_scalar_prefetch=1,
+            grid=(groups, views),
+            in_specs=[
+                pl.BlockSpec(
+                    block,
+                    lambda g, v, at: (
+                        lax.rem(at[0] - v + views, views),
+                        lax.rem(at[1] - g + groups, groups),
+                        0,
+                        0,
+                    ),
+                )
+            ],
+            out_specs=pl.BlockSpec(block, lambda g, v, at: (g, v, 0, 0)),
+        ),
+        out_shape=jax.ShapeDtypeStruct((groups, views, share, columns), rows.dtype),
+        compiler_params=pltpu.CompilerParams(vmem_limit_bytes=16 * 2**20),
+    )(at, stack)
+    return ordered.reshape(groups, views * share, columns)
+
+
 def local(query, key, value, out_weight, pairs, counts):
     views = lax.axis_size("view")
     groups = lax.axis_size("head")
     me = lax.axis_index("view")
     features = query.shape[1]
     heads = features // HEAD_DIM
-    chunks = 3 if heads % 3 == 0 else 1
-    per = heads // chunks
-    width = per * HEAD_DIM
+    sizes = [1] * min(heads, 2) + [2] * ((heads - 2) // 2) + [1] * (max(heads - 2, 0) % 2)
+    starts = [sum(sizes[:c]) for c in range(len(sizes))]
 
     slot_rows = pairs[0]
     live_count = lax.dynamic_index_in_dim(counts, me, 0, keepdims=True)
@@ -135,25 +188,23 @@
     source_tiles = jnp.sum(jnp.where(match, own_tiles[:, None], 0), axis=0)
     meta = jnp.concatenate([live_count, own_tiles, peers])
 
-    incoming = [
-        lax.all_to_all(
-            collect(source_tiles, key, value, c, width), "view", 0, 0, tiled=True
-        )
-        for c in range(chunks)
+    outgoing = [
+        collect(source_tiles, key, value, start // size, size * HEAD_DIM)
+        for start, size in zip(starts, sizes)
     ]
-    share = features // views
-    mine = lax.dynamic_slice_in_dim(out_weight, me * share, share, 0)
-    mine = lax.all_to_all(
-        mine.reshape(share, groups, -1), "head", split_axis=1, concat_axis=1, tiled=True
-    )
-    weight = lax.all_gather(mine, "view", axis=0, tiled=True)
+    rows = weight_rows(out_weight)
+    if len(sizes) > 1:
+        rows, outgoing[1] = lax.optimization_barrier((rows, outgoing[1]))
+    incoming = [lax.all_to_all(block, "view", 0, 0, tiled=True) for block in outgoing]
+    rows, incoming[-1] = lax.optimization_barrier((rows, incoming[-1]))
+    weight = spread_weight(rows)
 
     total = None
-    for c in range(chunks):
-        attended = attend(meta, query, key, value, incoming[c], c, per)
-        gathered = lax.all_gather(attended, "head", axis=0, tiled=False)
-        gathered = gathered.reshape(groups * width, -1)
-        part = jnp.swapaxes(weight[c * width : (c + 1) * width], 0, 1)
+    for start, size, block in zip(starts, sizes, incoming):
+        width = size * HEAD_DIM
+        attended = attend(meta, query, key, value, block, start, size)
+        gathered = lax.all_gather(attended, "head", axis=0, tiled=True)
+        part = weight[:, start * HEAD_DIM : start * HEAD_DIM + width]
         term = lax.dot_general(
             part.reshape(groups * width, -1),
             gathered,

time: 317 us -> 290 us (0.915)
  blocking collectives: 104 us -> 48 us
  starting transfers between devices: 4.58 us -> 33.7 us
  waiting for transfers between devices: 101 us -> 89.7 us
  matrix products: 21.8 us -> 27 us
    all_to_all x3 -> x1, blocking collectives: 104 us -> 48 us  [local(): lax.all_to_all(block, 'view', 0, 0, tiled=True)]
    ppermute x0 -> x10, waiting for transfers between devices: none -> 39.5 us  [shift(): lax.ppermute(array, axis, [(i, (i + step) % size) for i in range(size)])]
    all_gather x4, waiting for transfers between devices: 49.4 us -> 14.9 us  [local(): gathered = lax.all_gather(attended, 'head', axis=0, tiled=True)]
    ppermute x0 -> x10, starting transfers between devices: none -> 19.7 us  [shift(): lax.ppermute(array, axis, [(i, (i + step) % size) for i in range(size)])]
    all_to_all x1 -> x3, waiting for transfers between devices: 51.9 us -> 35.2 us  [local(): lax.all_to_all(block, 'view', 0, 0, tiled=True)]
    all_to_all x1 -> x3, starting transfers between devices: 4.45 us -> 13.9 us  [local(): lax.all_to_all(block, 'view', 0, 0, tiled=True)]
    dot_general x3 -> x4, matrix products: 21.8 us -> 27 us  [local(): lax.dot_general(part.reshape(groups * width, -1), gathered, (((0,), (0,))...]
    unnamed x31 -> x41, local copies, waits for them, and re-layouts: 20 us -> 23.7 us
  transfers between devices with their start and end apart: 5 -> 17, of which waited for: 2 -> 8; matrix products, arithmetic and copies ran while one was open for 10% -> 8% of each run, Pallas kernels for 13% -> 15%
where the time goes in v3:
time: 290 us; the launch traced here: 287 us
  waiting for transfers between devices  89.7 us (31%)
  blocking collectives  48 us (17%)
  Pallas kernels  45 us (16%)
  starting transfers between devices  33.7 us (12%)
  local copies, waits for them, and re-layouts  28.7 us (10%)
  matrix products  27 us (9%)
  between operations  13.4 us (5%)
    all_to_all x1, blocking collectives, local(): lax.all_to_all(block, 'view', 0, 0, tiled=True)  48 us
    ppermute x10, waiting for transfers between devices, shift(): lax.ppermute(array, axis, [(i, (i + step) % size) for i in range(size)])  39.5 us
    pallas_call x4, Pallas kernels, attend(): pl.pallas_call(functools.partial(attend_kernel, slots, tile), grid_spec=p...  38.3 us
    all_to_all x3, waiting for transfers between devices, local(): lax.all_to_all(block, 'view', 0, 0, tiled=True)  35.2 us
    dot_general x4, matrix products, local(): lax.dot_general(part.reshape(groups * width, -1), gathered, (((0,), (0,))...  27 us
    unnamed x41, local copies, waits for them, and re-layouts  23.7 us
    ppermute x10, starting transfers between devices, shift(): lax.ppermute(array, axis, [(i, (i + step) % size) for i in range(size)])  19.7 us
    all_gather x4, waiting for transfers between devices, local(): gathered = lax.all_gather(attended, 'head', axis=0, tiled=True)  14.9 us
  transfers between devices with their start and end apart: 17, of which 8 were waited for; matrix products, arithmetic and copies ran while one was open for 8% of the time, Pallas kernels for 15%

profile of v3, /device:TPU:0, one launch (start us, length us, event | category | flops | bytes accessed | tf_op | source)
XLA Modules:
  0.0 286.9 jit_solution(7555313364553882411)
XLA Ops:
  7.3 1.2 dynamic_slice.21
  9.2 1.7 copy-done
  10.9 1.7 copy-done.2
  12.5 1.3 shard_map.67
  13.9 1.1 copy-done.16
  15.0 5.1 %all-to-all-start.1 = ((bf16[8,384,256]{2,1,0:T(8,128)(2,1)}), bf16[8,384,256]{2,1,0:T(8,128)(2,1)}, u32[]{:S(2)}, u32[]{:S(2)}) async-start(bf16[8,384,256]{2,1,0:T(8,128)(2,1)} %copy-done.16), calls=%async_computation.1 | async-start | bytes 3145728 | tf_op jit(solution)/shard_map/all_to_all | solution.py:198
  20.1 1.7 copy-done.3
  21.8 1.2 shard_map.65
  23.0 1.7 copy-done.14
  24.7 16.6 %all-to-all-done.1.pk_ref.pv_ref = bf16[8,384,256]{2,1,0:T(8,128)(2,1)} async-done(((bf16[8,384,256]{2,1,0:T(8,128)(2,1)}), bf16[8,384,256]{2,1,0:T(8,128)(2,1)}, u32[]{:S(2)}, u32[]{:S(2)}) %all-to-all-start.1) | async-done | bytes 1572896 | tf_op jit(solution)/shard_map/all_to_all | solution.py:198
  41.3 4.4 %all-to-all-start = ((bf16[8,384,512]{2,1,0:T(8,128)(2,1)}), bf16[8,384,512]{2,1,0:T(8,128)(2,1)}, u32[]{:S(2)}, u32[]{:S(2)}) async-start(bf16[8,384,512]{2,1,0:T(8,128)(2,1)} %copy-done.14), calls=%async_computation | async-start | bytes 6291456 | tf_op jit(solution)/shard_map/all_to_all | solution.py:198
  46.4 1.7 copy-done.4
  48.1 1.7 copy-done.10
  49.7 7.4 %shard_map.68 = bf16[128,1536]{1,0:T(8,128)(2,1)} custom-call(s32[15]{0:T(128)S(1)} %pad_add_fusion.1.meta_ref, bf16[1536,768]{1,0:T(8,128)(2,1)S(1)} %copy-done.10, bf16[1536,768]{1,0:T(8,128)(2,1)S(1)} %copy-done.1, bf16[1536,768]{1,0:T(8,128)(2,1)S(1)} %copy-done.4, bf16[8,384,256]{2,1,0:T(8,128)(2,1)} %all-to-all-done.1.pk_ref.pv_ref, ...), custom_call_target="tpu_custom_call" | custom-call | flops 1660944384 | bytes 3145728 | tf_op jit(solution)/shard_map/pallas_call | solution.py:97
  57.3 1.6 dynamic-slice_bitcast_fusion
  58.8 4.2 %collective-permute-start.2 = (bf16[96,768]{1,0:T(8,128)(2,1)S(1)}, bf16[96,768]{1,0:T(8,128)(2,1)S(1)}, u32[]{:S(2)}, u32[]{:S(2)}) collective-permute-start(bf16[96,768]{1,0:T(8,128)(2,1)S(1)} %get-tuple-element.19), channel_id=1, source_target_pairs={{0,3},{1,0},{2,1},{3,2},{4,7},{5,4},{6,5},{7,6},{8,11},{9,8},{10,9... | collective-permute-start | bytes 442376 | tf_op jit(solution)/shard_map/ppermute | solution.py:122
  63.0 1.0 collective-permute-start
  64.0 1.7 copy-done.5
  65.7 1.3 shard_map.64
  67.0 1.1 copy-done.15
  68.2 15.1 %collective-permute-done.1 = bf16[96,768]{1,0:T(8,128)(2,1)S(1)} collective-permute-done((bf16[96,768]{1,0:T(8,128)(2,1)S(1)}, bf16[96,768]{1,0:T(8,128)(2,1)S(1)}, u32[]{:S(2)}, u32[]{:S(2)}) %collective-permute-start.1) | collective-permute-done | bytes 147488 | tf_op jit(solution)/shard_map/ppermute | solution.py:122
  83.6 1.7 copy-done.6
  85.3 1.7 copy-done.11
  87.0 12.1 %shard_map.72 = bf16[256,1536]{1,0:T(8,128)(2,1)} custom-call(s32[15]{0:T(128)S(1)} %pad_add_fusion.1.meta_ref, bf16[1536,768]{1,0:T(8,128)(2,1)S(1)} %copy-done.11, bf16[1536,768]{1,0:T(8,128)(2,1)S(1)} %copy-done.1, bf16[1536,768]{1,0:T(8,128)(2,1)S(1)} %copy-done.6, bf16[8,384,512]{2,1,0:T(8,128)(2,1)} %all-to-all-done.pk_ref.pv_ref, ...), custom_call_target="tpu_custom_call" | custom-call | flops 3321888768 | bytes 6291456 | tf_op jit(solution)/shard_map/pallas_call | solution.py:97
  99.1 1.7 copy-done.7
  100.8 1.2 shard_map.70
  102.0 48.0 %all_to_all.20.pk_ref.pv_ref = bf16[8,384,512]{2,1,0:T(8,128)(2,1)S(1)} all-to-all(bf16[8,384,512]{2,1,0:T(8,128)(2,1)S(1)} %shard_map.70), channel_id=1, replica_groups=mesh['view'=8,'head'=4] {'view'}, dimensions={0} | all-to-all | bytes 6291456 | tf_op jit(solution)/shard_map/all_to_all | solution.py:198
  150.0 11.4 %shard_map.71 = bf16[256,1536]{1,0:T(8,128)(2,1)} custom-call(s32[15]{0:T(128)S(1)} %pad_add_fusion.1.meta_ref, bf16[1536,768]{1,0:T(8,128)(2,1)S(1)} %copy-done.12, bf16[1536,768]{1,0:T(8,128)(2,1)S(1)} %copy-done.1, bf16[1536,768]{1,0:T(8,128)(2,1)S(1)} %copy-done.8, bf16[8,384,512]{2,1,0:T(8,128)(2,1)S(1)} %all_to_all.20.pk_ref.pv_ref, ...), custom_call_target="tpu_custom_call" | custom-call | flops 3321888768 | bytes 6291456 | tf_op jit(solution)/shard_map/pallas_call | solution.py:97
  161.5 4.3 %all-to-all-start.2 = ((bf16[8,384,256]{2,1,0:T(8,128)(2,1)}), bf16[8,384,256]{2,1,0:T(8,128)(2,1)}, u32[]{:S(2)}, u32[]{:S(2)}) async-start(bf16[8,384,256]{2,1,0:T(8,128)(2,1)} %copy-done.15), calls=%async_computation.2 | async-start | bytes 3145728 | tf_op jit(solution)/shard_map/all_to_all | solution.py:198
  166.2 2.6 collective-permute-start.4
  168.8 18.5 %all-to-all-done.2.pk_ref.pv_ref = bf16[8,384,256]{2,1,0:T(8,128)(2,1)} async-done(((bf16[8,384,256]{2,1,0:T(8,128)(2,1)}), bf16[8,384,256]{2,1,0:T(8,128)(2,1)}, u32[]{:S(2)}, u32[]{:S(2)}) %all-to-all-start.2) | async-done | bytes 1572896 | tf_op jit(solution)/shard_map/all_to_all | solution.py:198
  187.3 1.7 copy-done.9
  189.0 1.7 copy-done.13
  190.6 7.4 %shard_map.69 = bf16[128,1536]{1,0:T(8,128)(2,1)} custom-call(s32[15]{0:T(128)S(1)} %pad_add_fusion.1.meta_ref, bf16[1536,768]{1,0:T(8,128)(2,1)S(1)} %copy-done.13, bf16[1536,768]{1,0:T(8,128)(2,1)S(1)} %copy-done.1, bf16[1536,768]{1,0:T(8,128)(2,1)S(1)} %copy-done.9, bf16[8,384,256]{2,1,0:T(8,128)(2,1)} %all-to-all-done.2.pk_ref.pv_ref, ...), custom_call_target="tpu_custom_call" | custom-call | flops 1660944384 | bytes 3145728 | tf_op jit(solution)/shard_map/pallas_call | solution.py:97
  198.2 1.0 collective-permute-start.6
  199.2 1.4 collective-permute-start.7
  200.7 1.7 collective-permute-start.8
  202.4 1.1 bitcast_dynamic-update-slice_fusion.6
  203.5 7.3 %collective-permute-start.9 = (bf16[4,96,768]{2,1,0:T(8,128)(2,1)S(1)}, bf16[4,96,768]{2,1,0:T(8,128)(2,1)S(1)}, u32[]{:S(2)}, u32[]{:S(2)}) collective-permute-start(bf16[4,96,768]{2,1,0:T(8,128)(2,1)S(1)} %pad_maximum_fusion), channel_id=1, source_target_pairs={{0,28},{4,0},{8,4},{12,8},{16,12},{20,16},{24,20},{28,24},{1,29},{... | collective-permute-start | bytes 1769480 | tf_op jit(solution)/shard_map/ppermute | solution.py:122
  210.9 13.7 %collective-permute-done.5 = bf16[4,96,768]{2,1,0:T(8,128)(2,1)S(1)} collective-permute-done((bf16[4,96,768]{2,1,0:T(8,128)(2,1)S(1)}, bf16[4,96,768]{2,1,0:T(8,128)(2,1)S(1)}, u32[]{:S(2)}, u32[]{:S(2)}) %collective-permute-start.5) | collective-permute-done | bytes 589856 | tf_op jit(solution)/shard_map/ppermute | solution.py:122
  224.7 10.6 %collective-permute-done.7 = bf16[4,96,768]{2,1,0:T(8,128)(2,1)S(1)} collective-permute-done((bf16[4,96,768]{2,1,0:T(8,128)(2,1)S(1)}, bf16[4,96,768]{2,1,0:T(8,128)(2,1)S(1)}, u32[]{:S(2)}, u32[]{:S(2)}) %collective-permute-start.7) | collective-permute-done | bytes 589856 | tf_op jit(solution)/shard_map/ppermute | solution.py:122
  235.5 1.6 shard_map.66
  237.2 1.3 fusion.2
  238.6 5.0 %fusion.3 = f32[768,1536]{1,0:T(8,128)} fusion(bf16[512,768]{1,0:T(8,128)(2,1)S(1)} %bitcast.47, bf16[512,1536]{1,0:T(8,128)(2,1)} %all-gather.5.cloned.1.call-done), kind=kOutput, calls=%fused_computation.21 | convolution fusion | flops 1207959552 | bytes 7077888 | tf_op jit(solution)/shard_map/dot_general | solution.py:208
  243.5 7.2 %fusion.5 = f32[768,1536]{1,0:T(8,128)} fusion(bf16[1024,768]{1,0:T(8,128)(2,1)} %bitcast.45, bf16[1024,1536]{1,0:T(8,128)(2,1)} %all-gather.11.cloned.1.call-done), kind=kOutput, calls=%fused_computation.23 | convolution fusion | flops 2415919104 | bytes 9437184 | tf_op jit(solution)/shard_map/dot_general | solution.py:208
  250.7 6.2 %fusion.4 = f32[768,1536]{1,0:T(8,128)} fusion(bf16[1024,768]{1,0:T(8,128)(2,1)S(1)} %bitcast.44, bf16[1024,1536]{1,0:T(8,128)(2,1)} %all-gather.9.cloned.1.call-done), kind=kOutput, calls=%fused_computation.22 | convolution fusion | flops 2415919104 | bytes 9437184 | tf_op jit(solution)/shard_map/dot_general | solution.py:208
  256.9 14.9 %all-gather.7.cloned.1.call-done = bf16[512,1536]{1,0:T(8,128)(2,1)} async-done(((bf16[128,1536]{1,0:T(8,128)(2,1)}), bf16[512,1536]{1,0:T(8,128)(2,1)}) %all-gather.7.cloned.1.call-update) | async-done | bytes 1572880 | tf_op jit(solution)/shard_map/all_gather | solution.py:206
  271.8 8.6 %add_convert_fusion = bf16[768,1536]{1,0:T(8,128)(2,1)} fusion(f32[768,1536]{1,0:T(8,128)} %fusion.5, f32[768,1536]{1,0:T(8,128)} %fusion.4, f32[768,1536]{1,0:T(8,128)} %fusion.3, bf16[512,768]{1,0:T(8,128)(2,1)S(1)} %bitcast.46, bf16[512,1536]{1,0:T(8,128)(2,1)} %all-gather.7.cloned.1.call-done), kind=kOutput, calls=%fused_computation | convolution fusion | flops 1212678144 | bytes 18874368 | tf_op jit(solution)/shard_map/dot_general | solution.py:208
  (56 shorter events, 3.6 us)
Async XLA Ops:
  9.2 1.7 copy-start
  10.8 1.7 copy-start.2
  12.5 7.6 %copy-start.1 = (bf16[1536,768]{1,0:T(8,128)(2,1)S(1)}, bf16[1536,768]{1,0:T(8,128)(2,1)}, u32[]{:S(2)}) copy-start(bf16[1536,768]{1,0:T(8,128)(2,1)} %k_ref.7) | copy-start | bytes 7077892
  13.8 1.1 copy-start.16
  15.0 26.3 %all-to-all-start.1 = ((bf16[8,384,256]{2,1,0:T(8,128)(2,1)}), bf16[8,384,256]{2,1,0:T(8,128)(2,1)}, u32[]{:S(2)}, u32[]{:S(2)}) async-start(bf16[8,384,256]{2,1,0:T(8,128)(2,1)} %copy-done.16), calls=%async_computation.1 | async-start | bytes 3145728 | tf_op jit(solution)/shard_map/all_to_all | solution.py:198
  20.1 1.7 copy-start.3
  23.0 1.7 copy-start.14
  41.3 42.3 %all-to-all-start = ((bf16[8,384,512]{2,1,0:T(8,128)(2,1)}), bf16[8,384,512]{2,1,0:T(8,128)(2,1)}, u32[]{:S(2)}, u32[]{:S(2)}) async-start(bf16[8,384,512]{2,1,0:T(8,128)(2,1)} %copy-done.14), calls=%async_computation | async-start | bytes 6291456 | tf_op jit(solution)/shard_map/all_to_all | solution.py:198
  45.7 192.9 %all-gather.5.cloned.1.call-start = ((), (), s32[]{:S(2)}) async-start(), calls=%async_computation.4 | async-start | bytes 1966080 | tf_op jit(solution)/shard_map/all_gather | solution.py:206
  46.4 1.7 copy-start.4
  48.1 1.7 copy-start.10
  57.2 186.4 %all-gather.11.cloned.1.call-start = ((), (), s32[]{:S(2)}) async-start(), calls=%async_computation.7 | async-start | bytes 3932160 | tf_op jit(solution)/shard_map/all_gather | solution.py:206
  58.8 9.3 %collective-permute-start.2 = (bf16[96,768]{1,0:T(8,128)(2,1)S(1)}, bf16[96,768]{1,0:T(8,128)(2,1)S(1)}, u32[]{:S(2)}, u32[]{:S(2)}) collective-permute-start(bf16[96,768]{1,0:T(8,128)(2,1)S(1)} %get-tuple-element.19), channel_id=1, source_target_pairs={{0,3},{1,0},{2,1},{3,2},{4,7},{5,4},{6,5},{7,6},{8,11},{9,8},{10,9... | collective-permute-start | bytes 442376 | tf_op jit(solution)/shard_map/ppermute | solution.py:122
  63.0 20.3 %collective-permute-start.1 = (bf16[96,768]{1,0:T(8,128)(2,1)S(1)}, bf16[96,768]{1,0:T(8,128)(2,1)S(1)}, u32[]{:S(2)}, u32[]{:S(2)}) collective-permute-start(bf16[96,768]{1,0:T(8,128)(2,1)S(1)} %get-tuple-element.20), channel_id=1, source_target_pairs={{0,2},{1,3},{2,0},{3,1},{4,6},{5,7},{6,4},{7,5},{8,10},{9,11},{10,... | collective-permute-start | bytes 442376 | tf_op jit(solution)/shard_map/ppermute | solution.py:122
  63.0 20.3 %collective-permute-start = (bf16[96,768]{1,0:T(8,128)(2,1)S(1)}, bf16[96,768]{1,0:T(8,128)(2,1)S(1)}, u32[]{:S(2)}, u32[]{:S(2)}) collective-permute-start(bf16[96,768]{1,0:T(8,128)(2,1)S(1)} %get-tuple-element.18), channel_id=1, source_target_pairs={{0,1},{1,2},{2,3},{3,0},{4,5},{5,6},{6,7},{7,4},{8,9},{9,10},{10,1... | collective-permute-start | bytes 442376 | tf_op jit(solution)/shard_map/ppermute | solution.py:122
  64.0 1.7 copy-start.5
  67.0 1.1 copy-start.15
  83.6 1.7 copy-start.6
  85.3 1.7 copy-start.11
  99.1 151.7 %all-gather.9.cloned.1.call-start = ((), (), s32[]{:S(2)}) async-start(), calls=%async_computation.6 | async-start | bytes 3932160 | tf_op jit(solution)/shard_map/all_gather | solution.py:206
  99.1 1.7 copy-start.7
  102.0 48.0 %copy-start.8 = (bf16[1536,768]{1,0:T(8,128)(2,1)S(1)}, bf16[1536,768]{1,0:T(8,128)(2,1)}, u32[]{:S(2)}) copy-start(bf16[1536,768]{1,0:T(8,128)(2,1)} %v_ref.7) | copy-start | bytes 7077892
  102.0 48.0 %copy-start.12 = (bf16[1536,768]{1,0:T(8,128)(2,1)S(1)}, bf16[1536,768]{1,0:T(8,128)(2,1)}, u32[]{:S(2)}) copy-start(bf16[1536,768]{1,0:T(8,128)(2,1)} %q_ref.7) | copy-start | bytes 7077892
  161.5 25.8 %all-to-all-start.2 = ((bf16[8,384,256]{2,1,0:T(8,128)(2,1)}), bf16[8,384,256]{2,1,0:T(8,128)(2,1)}, u32[]{:S(2)}, u32[]{:S(2)}) async-start(bf16[8,384,256]{2,1,0:T(8,128)(2,1)} %copy-done.15), calls=%async_computation.2 | async-start | bytes 3145728 | tf_op jit(solution)/shard_map/all_to_all | solution.py:198
  165.8 106.0 %all-gather.7.cloned.1.call-start = ((), (), s32[]{:S(2)}) async-start(), calls=%async_computation.5 | async-start | bytes 1966080 | tf_op jit(solution)/shard_map/all_gather | solution.py:206
  165.8 34.8 %collective-permute-start.3 = (bf16[4,96,768]{2,1,0:T(8,128)(2,1)S(1)}, bf16[4,96,768]{2,1,0:T(8,128)(2,1)}, u32[]{:S(2)}, u32[]{:S(2)}) collective-permute-start(bf16[4,96,768]{2,1,0:T(8,128)(2,1)S(1)} %pad_maximum_fusion), channel_id=1, source_target_pairs={{0,4},{4,8},{8,12},{12,16},{16,20},{20,24},{24,28},{28,0},{1,5},{5... | collective-permute-start | bytes 1769480 | tf_op jit(solution)/shard_map/ppermute | solution.py:122
  166.2 37.2 %collective-permute-start.4 = (bf16[4,96,768]{2,1,0:T(8,128)(2,1)S(1)}, bf16[4,96,768]{2,1,0:T(8,128)(2,1)S(1)}, u32[]{:S(2)}, u32[]{:S(2)}) collective-permute-start(bf16[4,96,768]{2,1,0:T(8,128)(2,1)S(1)} %pad_maximum_fusion), channel_id=1, source_target_pairs={{0,8},{4,12},{8,16},{12,20},{16,24},{20,28},{24,0},{28,4},{1,9},{5... | collective-permute-start | bytes 1769480 | tf_op jit(solution)/shard_map/ppermute | solution.py:122
  187.3 1.7 copy-start.9
  189.0 1.7 copy-start.13
  198.1 26.5 %collective-permute-start.5 = (bf16[4,96,768]{2,1,0:T(8,128)(2,1)S(1)}, bf16[4,96,768]{2,1,0:T(8,128)(2,1)S(1)}, u32[]{:S(2)}, u32[]{:S(2)}) collective-permute-start(bf16[4,96,768]{2,1,0:T(8,128)(2,1)S(1)} %pad_maximum_fusion), channel_id=1, source_target_pairs={{0,12},{4,16},{8,20},{12,24},{16,28},{20,0},{24,4},{28,8},{1,13},{... | collective-permute-start | bytes 1769480 | tf_op jit(solution)/shard_map/ppermute | solution.py:122
  198.2 26.5 %collective-permute-start.6 = (bf16[4,96,768]{2,1,0:T(8,128)(2,1)S(1)}, bf16[4,96,768]{2,1,0:T(8,128)(2,1)S(1)}, u32[]{:S(2)}, u32[]{:S(2)}) collective-permute-start(bf16[4,96,768]{2,1,0:T(8,128)(2,1)S(1)} %pad_maximum_fusion), channel_id=1, source_target_pairs={{0,16},{4,20},{8,24},{12,28},{16,0},{20,4},{24,8},{28,12},{1,17},{... | collective-permute-start | bytes 1769480 | tf_op jit(solution)/shard_map/ppermute | solution.py:122
  199.2 36.1 %collective-permute-start.7 = (bf16[4,96,768]{2,1,0:T(8,128)(2,1)S(1)}, bf16[4,96,768]{2,1,0:T(8,128)(2,1)S(1)}, u32[]{:S(2)}, u32[]{:S(2)}) collective-permute-start(bf16[4,96,768]{2,1,0:T(8,128)(2,1)S(1)} %pad_maximum_fusion), channel_id=1, source_target_pairs={{0,20},{4,24},{8,28},{12,0},{16,4},{20,8},{24,12},{28,16},{1,21},{... | collective-permute-start | bytes 1769480 | tf_op jit(solution)/shard_map/ppermute | solution.py:122
  200.7 34.7 %collective-permute-start.8 = (bf16[4,96,768]{2,1,0:T(8,128)(2,1)S(1)}, bf16[4,96,768]{2,1,0:T(8,128)(2,1)S(1)}, u32[]{:S(2)}, u32[]{:S(2)}) collective-permute-start(bf16[4,96,768]{2,1,0:T(8,128)(2,1)S(1)} %pad_maximum_fusion), channel_id=1, source_target_pairs={{0,24},{4,28},{8,0},{12,4},{16,8},{20,12},{24,16},{28,20},{1,25},{... | collective-permute-start | bytes 1769480 | tf_op jit(solution)/shard_map/ppermute | solution.py:122
  203.5 32.0 %collective-permute-start.9 = (bf16[4,96,768]{2,1,0:T(8,128)(2,1)S(1)}, bf16[4,96,768]{2,1,0:T(8,128)(2,1)S(1)}, u32[]{:S(2)}, u32[]{:S(2)}) collective-permute-start(bf16[4,96,768]{2,1,0:T(8,128)(2,1)S(1)} %pad_maximum_fusion), channel_id=1, source_target_pairs={{0,28},{4,0},{8,4},{12,8},{16,12},{20,16},{24,20},{28,24},{1,29},{... | collective-permute-start | bytes 1769480 | tf_op jit(solution)/shard_map/ppermute | solution.py:122
Sparse Core Ops, SparseCore 0:
  57.3 43.6 all-gather.4
  102.6 68.2 all-gather.10
  172.4 62.1 all-gather.8
  236.0 35.7 all-gather.6

commit v4 on v3

--- a/solution.py
+++ b/solution.py
@@ -125,9 +125,10 @@
 def weight_rows(out_weight):
     groups = lax.axis_size("head")
     view, group = lax.axis_index("view"), lax.axis_index("head")
-    share = out_weight.shape[0] // lax.axis_size("view")
+    pair = math.gcd(lax.axis_size("view"), 2)
+    share = out_weight.shape[0] // pair
     columns = out_weight.shape[1] // groups
-    mine = lax.dynamic_slice_in_dim(out_weight, view * share, share, 0)
+    mine = lax.dynamic_slice_in_dim(out_weight, lax.rem(view, pair) * share, share, 0)
     blocks = []
     for step in range(groups):
         block = lax.dynamic_slice_in_dim(
@@ -143,20 +144,24 @@
 
 def spread_weight(rows):
     views, groups = lax.axis_size("view"), lax.axis_size("head")
+    pair = math.gcd(views, 2)
     _, share, columns = rows.shape
-    stack = jnp.stack([rows] + [shift(rows, "view", step) for step in range(1, views)])
-    at = jnp.stack([lax.axis_index("view"), lax.axis_index("head")])
+    parts = [rows]
+    if pair == 2:
+        parts.append(lax.ppermute(rows, "view", [(i, i ^ 1) for i in range(views)]))
+    stack = jnp.stack(parts)
+    at = jnp.stack([lax.rem(lax.axis_index("view"), pair), lax.axis_index("head")])
     block = (1, 1, share, columns)
     ordered = pl.pallas_call(
         order_kernel,
         grid_spec=pltpu.PrefetchScalarGridSpec(
             num_scalar_prefetch=1,
-            grid=(groups, views),
+            grid=(groups, pair),
             in_specs=[
                 pl.BlockSpec(
                     block,
                     lambda g, v, at: (
-                        lax.rem(at[0] - v + views, views),
+                        lax.rem(at[0] - v + pair, pair),
                         lax.rem(at[1] - g + groups, groups),
                         0,
                         0,
@@ -165,10 +170,10 @@
             ],
             out_specs=pl.BlockSpec(block, lambda g, v, at: (g, v, 0, 0)),
         ),
-        out_shape=jax.ShapeDtypeStruct((groups, views, share, columns), rows.dtype),
+        out_shape=jax.ShapeDtypeStruct((groups, pair, share, columns), rows.dtype),
         compiler_params=pltpu.CompilerParams(vmem_limit_bytes=16 * 2**20),
     )(at, stack)
-    return ordered.reshape(groups, views * share, columns)
+    return ordered.reshape(groups, pair * share, columns)
 
 
 def local(query, key, value, out_weight, pairs, counts):
@@ -193,10 +198,8 @@
         for start, size in zip(starts, sizes)
     ]
     rows = weight_rows(out_weight)
-    if len(sizes) > 1:
-        rows, outgoing[1] = lax.optimization_barrier((rows, outgoing[1]))
     incoming = [lax.all_to_all(block, "view", 0, 0, tiled=True) for block in outgoing]
-    rows, incoming[-1] = lax.optimization_barrier((rows, incoming[-1]))
+    rows, incoming[0] = lax.optimization_barrier((rows, incoming[0]))
     weight = spread_weight(rows)
 
     total = None

time: 290 us -> 311 us (1.072)
  waiting for transfers between devices: 89.7 us -> 123 us
  starting transfers between devices: 33.7 us -> 20.3 us
  Pallas kernels: 45 us -> 53.5 us
  blocking collectives: 48 us -> 40.6 us
  other arithmetic: 1.43 us -> 8.01 us
  local copies, waits for them, and re-layouts: 28.7 us -> 24.2 us
    all_gather x4, waiting for transfers between devices: 14.9 us -> 69.6 us  [local(): gathered = lax.all_gather(attended, 'head', axis=0, tiled=True)]
    ppermute x10 -> x3, waiting for transfers between devices: 39.5 us -> 21.8 us  [shift(): lax.ppermute(array, axis, [(i, (i + step) % size) for i in range(size)])]
    ppermute x10 -> x3, starting transfers between devices: 19.7 us -> 6.15 us  [shift(): lax.ppermute(array, axis, [(i, (i + step) % size) for i in range(size)])]
    all_to_all x1, blocking collectives: 48 us -> 40.6 us  [local(): lax.all_to_all(block, 'view', 0, 0, tiled=True)]
    unnamed x41 -> x34, local copies, waits for them, and re-layouts: 23.7 us -> 16.2 us
    pallas_call x4, Pallas kernels: 38.3 us -> 45.5 us  [attend(): pl.pallas_call(functools.partial(attend_kernel, slots, tile), grid_spec=p...]
    all_to_all x3, waiting for transfers between devices: 35.2 us -> 32 us  [local(): lax.all_to_all(block, 'view', 0, 0, tiled=True)]
    another operation x1, other arithmetic: 0.08 us -> 3.27 us  [weight_rows(): return jnp.stack(blocks)]
  transfers between devices with their start and end apart: 17 -> 11, of which waited for: 8 -> 6; matrix products, arithmetic and copies ran while one was open for 8% -> 10% of each run, Pallas kernels for 15% -> 16%
where the time goes in v4:
time: 311 us; the launch traced here: 310 us
  waiting for transfers between devices  123 us (40%)
  Pallas kernels  53.5 us (17%)
  blocking collectives  40.6 us (13%)
  matrix products  26.3 us (8%)
  local copies, waits for them, and re-layouts  24.2 us (8%)
  starting transfers between devices  20.3 us (7%)
  between operations  13.3 us (4%)
  other arithmetic  8.01 us (3%)
    all_gather x4, waiting for transfers between devices, local(): gathered = lax.all_gather(attended, 'head', axis=0, tiled=True)  69.6 us
    pallas_call x4, Pallas kernels, attend(): pl.pallas_call(functools.partial(attend_kernel, slots, tile), grid_spec=p...  45.5 us
    all_to_all x1, blocking collectives, local(): lax.all_to_all(block, 'view', 0, 0, tiled=True)  40.6 us
    all_to_all x3, waiting for transfers between devices, local(): lax.all_to_all(block, 'view', 0, 0, tiled=True)  32 us
    dot_general x4, matrix products, local(): lax.dot_general(part.reshape(groups * width, -1), gathered, (((0,), (0,))...  26.3 us
    ppermute x3, waiting for transfers between devices, shift(): lax.ppermute(array, axis, [(i, (i + step) % size) for i in range(size)])  21.8 us
    unnamed x34, local copies, waits for them, and re-layouts  16.2 us
    all_to_all x3, starting transfers between devices, local(): lax.all_to_all(block, 'view', 0, 0, tiled=True)  13.9 us
  transfers between devices with their start and end apart: 11, of which 6 were waited for; matrix products, arithmetic and copies ran while one was open for 10% of the time, Pallas kernels for 16%

profile of v4, /device:TPU:0, one launch (start us, length us, event | category | flops | bytes accessed | tf_op | source)
XLA Modules:
  0.0 309.7 jit_solution(18266999714728312908)
XLA Ops:
  6.5 1.3 dynamic_slice.21
  7.8 0.7 iota_compare_fusion.1
  8.5 0.8 slice_bitcast_fusion.1
  9.3 0.1 select_reduce_fusion.source_ref
  9.4 1.7 copy-done
  11.1 1.7 copy-done.2
  12.7 3.6 %shard_map.64 = bf16[8,384,256]{2,1,0:T(8,128)(2,1)} custom-call(s32[8]{0:T(128)S(1)} %select_reduce_fusion.source_ref, bf16[1536,768]{1,0:T(8,128)(2,1)S(1)} %copy-done, bf16[1536,768]{1,0:T(8,128)(2,1)S(1)} %copy-done.2), custom_call_target="tpu_custom_call" | custom-call | bytes 3145728 | tf_op jit(solution)/shard_map/pallas_call | solution.py:26
  16.3 5.2 %all-to-all-start = ((bf16[8,384,256]{2,1,0:T(8,128)(2,1)}), bf16[8,384,256]{2,1,0:T(8,128)(2,1)}, u32[]{:S(2)}, u32[]{:S(2)}) async-start(bf16[8,384,256]{2,1,0:T(8,128)(2,1)} %shard_map.64), calls=%async_computation | async-start | bytes 3145728 | tf_op jit(solution)/shard_map/all_to_all | solution.py:201
  21.5 4.4 %dynamic-slice_bitcast_fusion = (bf16[1,384,768]{2,1,0:T(8,128)(2,1)S(1)}, bf16[384,768]{1,0:T(8,128)(2,1)}, bf16[384,768]{1,0:T(8,128)(2,1)S(1)}, bf16[384,768]{1,0:T(8,128)(2,1)}) fusion(bf16[768,3072]{1,0:T(8,128)(2,1)} %param.9, s32[]{:T(128)S(6)} %select_n.34, s32[]{:T(128)S(6)} %select_n.36, s32[]{:T(128)S(6)} %select_n.38, s32[]{:T(128)S(6)} %select_n.42, ...), kind=kLoop, calls=%fused_computation.3 | loop fusion | bytes 4718612 | tf_op jit(solution)/shard_map/stack | solution.py:138
  26.0 2.2 collective-permute-start
  28.2 2.6 collective-permute-start.1
  30.8 1.3 collective-permute-start.2
  32.1 1.1 shard_map.69
  33.2 1.7 copy-done.14
  34.9 7.7 %all-to-all-done.pk_ref.pv_ref = bf16[8,384,256]{2,1,0:T(8,128)(2,1)} async-done(((bf16[8,384,256]{2,1,0:T(8,128)(2,1)}), bf16[8,384,256]{2,1,0:T(8,128)(2,1)}, u32[]{:S(2)}, u32[]{:S(2)}) %all-to-all-start) | async-done | bytes 1572896 | tf_op jit(solution)/shard_map/all_to_all | solution.py:201
  42.6 4.5 %all-to-all-start.2 = ((bf16[8,384,512]{2,1,0:T(8,128)(2,1)}), bf16[8,384,512]{2,1,0:T(8,128)(2,1)}, u32[]{:S(2)}, u32[]{:S(2)}) async-start(bf16[8,384,512]{2,1,0:T(8,128)(2,1)} %copy-done.14), calls=%async_computation.2 | async-start | bytes 6291456 | tf_op jit(solution)/shard_map/all_to_all | solution.py:201
  47.2 0.8 pad_add_fusion.1.meta_ref
  47.9 21.8 %collective-permute-done.1 = bf16[384,768]{1,0:T(8,128)(2,1)} collective-permute-done((bf16[384,768]{1,0:T(8,128)(2,1)}, bf16[384,768]{1,0:T(8,128)(2,1)}, u32[]{:S(2)}, u32[]{:S(2)}) %collective-permute-start.1) | collective-permute-done | bytes 589856 | tf_op jit(solution)/shard_map/ppermute | solution.py:122
  69.7 3.3 %pad_maximum_fusion.1 = bf16[4,384,768]{2,1,0:T(8,128)(2,1)} fusion(bf16[1,384,768]{2,1,0:T(8,128)(2,1)} %bitcast.5, bf16[1,384,768]{2,1,0:T(8,128)(2,1)} %bitcast.4, bf16[1,384,768]{2,1,0:T(8,128)(2,1)} %bitcast.3, bf16[1,384,768]{2,1,0:T(8,128)(2,1)S(1)} %get-tuple-element.13), kind=kLoop, calls=%fused_computation.2 | loop fusion | flops 3538944 | bytes 4718592 | tf_op jit(solution)/shard_map/stack | solution.py:138
  73.0 8.6 %shard_map.66 = bf16[128,1536]{1,0:T(8,128)(2,1)} custom-call(s32[15]{0:T(128)S(1)} %pad_add_fusion.1.meta_ref, bf16[1536,768]{1,0:T(8,128)(2,1)S(1)} %copy-done.10, bf16[1536,768]{1,0:T(8,128)(2,1)S(1)} %copy-done.1, bf16[1536,768]{1,0:T(8,128)(2,1)S(1)} %copy-done.4, bf16[8,384,256]{2,1,0:T(8,128)(2,1)} %all-to-all-done.pk_ref.pv_ref, ...), custom_call_target="tpu_custom_call" | custom-call | flops 1660944384 | bytes 3145728 | tf_op jit(solution)/shard_map/pallas_call | solution.py:97
  81.7 3.3 %all-to-all-done.2.pk_ref.pv_ref = bf16[8,384,512]{2,1,0:T(8,128)(2,1)} async-done(((bf16[8,384,512]{2,1,0:T(8,128)(2,1)}), bf16[8,384,512]{2,1,0:T(8,128)(2,1)}, u32[]{:S(2)}, u32[]{:S(2)}) %all-to-all-start.2) | async-done | bytes 3145760 | tf_op jit(solution)/shard_map/all_to_all | solution.py:201
  85.0 1.7 copy-done.5
  86.7 1.7 copy-done.11
  88.3 14.4 %shard_map.70 = bf16[256,1536]{1,0:T(8,128)(2,1)} custom-call(s32[15]{0:T(128)S(1)} %pad_add_fusion.1.meta_ref, bf16[1536,768]{1,0:T(8,128)(2,1)S(1)} %copy-done.11, bf16[1536,768]{1,0:T(8,128)(2,1)S(1)} %copy-done.1, bf16[1536,768]{1,0:T(8,128)(2,1)S(1)} %copy-done.5, bf16[8,384,512]{2,1,0:T(8,128)(2,1)} %all-to-all-done.2.pk_ref.pv_ref, ...), custom_call_target="tpu_custom_call" | custom-call | flops 3321888768 | bytes 6291456 | tf_op jit(solution)/shard_map/pallas_call | solution.py:97
  102.8 1.7 copy-done.6
  104.5 1.1 shard_map.71
  105.6 40.6 %all_to_all.20.pk_ref.pv_ref = bf16[8,384,512]{2,1,0:T(8,128)(2,1)S(1)} all-to-all(bf16[8,384,512]{2,1,0:T(8,128)(2,1)S(1)} %shard_map.71), channel_id=1, replica_groups=mesh['view'=8,'head'=4] {'view'}, dimensions={0} | all-to-all | bytes 6291456 | tf_op jit(solution)/shard_map/all_to_all | solution.py:201
  146.1 13.8 %shard_map.72 = bf16[256,1536]{1,0:T(8,128)(2,1)} custom-call(s32[15]{0:T(128)S(1)} %pad_add_fusion.1.meta_ref, bf16[1536,768]{1,0:T(8,128)(2,1)S(1)} %copy-done.12, bf16[1536,768]{1,0:T(8,128)(2,1)S(1)} %copy-done.1, bf16[1536,768]{1,0:T(8,128)(2,1)S(1)} %copy-done.7, bf16[8,384,512]{2,1,0:T(8,128)(2,1)S(1)} %all_to_all.20.pk_ref.pv_ref, ...), custom_call_target="tpu_custom_call" | custom-call | flops 3321888768 | bytes 6291456 | tf_op jit(solution)/shard_map/pallas_call | solution.py:97
  159.9 0.1 collective-permute-start.3
  160.0 1.7 copy-done.8
  161.7 1.2 shard_map.67
  162.9 1.2 copy-done.15
  164.1 4.3 %all-to-all-start.1 = ((bf16[8,384,256]{2,1,0:T(8,128)(2,1)}), bf16[8,384,256]{2,1,0:T(8,128)(2,1)}, u32[]{:S(2)}, u32[]{:S(2)}) async-start(bf16[8,384,256]{2,1,0:T(8,128)(2,1)} %copy-done.15), calls=%async_computation.1 | async-start | bytes 3145728 | tf_op jit(solution)/shard_map/all_to_all | solution.py:201
  168.4 0.1 pad_add_fusion.at_ref
  168.5 20.9 %all-to-all-done.1.pk_ref.pv_ref = bf16[8,384,256]{2,1,0:T(8,128)(2,1)} async-done(((bf16[8,384,256]{2,1,0:T(8,128)(2,1)}), bf16[8,384,256]{2,1,0:T(8,128)(2,1)}, u32[]{:S(2)}, u32[]{:S(2)}) %all-to-all-start.1) | async-done | bytes 1572896 | tf_op jit(solution)/shard_map/all_to_all | solution.py:201
  189.4 1.7 copy-done.9
  191.1 1.7 copy-done.13
  192.8 8.7 %shard_map.68 = bf16[128,1536]{1,0:T(8,128)(2,1)} custom-call(s32[15]{0:T(128)S(1)} %pad_add_fusion.1.meta_ref, bf16[1536,768]{1,0:T(8,128)(2,1)S(1)} %copy-done.13, bf16[1536,768]{1,0:T(8,128)(2,1)S(1)} %copy-done.1, bf16[1536,768]{1,0:T(8,128)(2,1)S(1)} %copy-done.9, bf16[8,384,256]{2,1,0:T(8,128)(2,1)} %all-to-all-done.1.pk_ref.pv_ref, ...), custom_call_target="tpu_custom_call" | custom-call | flops 1660944384 | bytes 3145728 | tf_op jit(solution)/shard_map/pallas_call | solution.py:97
  201.5 3.1 %pad_maximum_fusion.in_ref = bf16[2,4,384,768]{3,2,1,0:T(8,128)(2,1)S(1)} fusion(bf16[1,4,384,768]{3,2,1,0:T(8,128)(2,1)} %bitcast.11, bf16[1,4,384,768]{3,2,1,0:T(8,128)(2,1)} %bitcast.30), kind=kLoop, calls=%fused_computation | loop fusion | flops 2359296 | bytes 9437184 | tf_op jit(solution)/shard_map/stack | solution.py:152
  204.7 1.1 shard_map.65
  205.7 1.3 fusion.1
  207.0 0.2 fusion.2
  207.3 5.2 %fusion.3 = f32[768,1536]{1,0:T(8,128)} fusion(bf16[512,768]{1,0:T(8,128)(2,1)} %bitcast.34, bf16[512,1536]{1,0:T(8,128)(2,1)} %all-gather.5.cloned.1.call-done), kind=kOutput, calls=%fused_computation.14 | convolution fusion | flops 1207959552 | bytes 7077888 | tf_op jit(solution)/shard_map/dot_general | solution.py:211
  212.5 6.2 %fusion.4 = f32[768,1536]{1,0:T(8,128)} fusion(bf16[1024,768]{1,0:T(8,128)(2,1)S(1)} %bitcast.32, bf16[1024,1536]{1,0:T(8,128)(2,1)} %all-gather.9.cloned.1.call-done), kind=kOutput, calls=%fused_computation.15 | convolution fusion | flops 2415919104 | bytes 9437184 | tf_op jit(solution)/shard_map/dot_general | solution.py:211
  218.7 38.7 %all-gather.11.cloned.1.call-done = bf16[1024,1536]{1,0:T(8,128)(2,1)} async-done(((bf16[256,1536]{1,0:T(8,128)(2,1)}), bf16[1024,1536]{1,0:T(8,128)(2,1)}) %all-gather.11.cloned.1.call-update) | async-done | bytes 3145744 | tf_op jit(solution)/shard_map/all_gather | solution.py:209
  257.4 6.2 %fusion.5 = f32[768,1536]{1,0:T(8,128)} fusion(bf16[1024,768]{1,0:T(8,128)(2,1)S(1)} %bitcast.31, bf16[1024,1536]{1,0:T(8,128)(2,1)} %all-gather.11.cloned.1.call-done), kind=kOutput, calls=%fused_computation.16 | convolution fusion | flops 2415919104 | bytes 9437184 | tf_op jit(solution)/shard_map/dot_general | solution.py:211
  263.6 31.0 %all-gather.7.cloned.1.call-done = bf16[512,1536]{1,0:T(8,128)(2,1)} async-done(((bf16[128,1536]{1,0:T(8,128)(2,1)}), bf16[512,1536]{1,0:T(8,128)(2,1)}) %all-gather.7.cloned.1.call-update) | async-done | bytes 1572880 | tf_op jit(solution)/shard_map/all_gather | solution.py:209
  294.6 8.6 %add_convert_fusion = bf16[768,1536]{1,0:T(8,128)(2,1)} fusion(f32[768,1536]{1,0:T(8,128)} %fusion.5, f32[768,1536]{1,0:T(8,128)} %fusion.4, f32[768,1536]{1,0:T(8,128)} %fusion.3, bf16[512,768]{1,0:T(8,128)(2,1)S(1)} %bitcast.33, bf16[512,1536]{1,0:T(8,128)(2,1)} %all-gather.7.cloned.1.call-done), kind=kOutput, calls=%fused_computation.1 | convolution fusion | flops 1212678144 | bytes 18874368 | tf_op jit(solution)/shard_map/dot_general | solution.py:211
  (37 shorter events, 0.3 us)
Async XLA Ops:
  9.4 1.7 copy-start
  11.1 1.7 copy-start.2
  16.3 26.3 %all-to-all-start = ((bf16[8,384,256]{2,1,0:T(8,128)(2,1)}), bf16[8,384,256]{2,1,0:T(8,128)(2,1)}, u32[]{:S(2)}, u32[]{:S(2)}) async-start(bf16[8,384,256]{2,1,0:T(8,128)(2,1)} %shard_map.64), calls=%async_computation | async-start | bytes 3145728 | tf_op jit(solution)/shard_map/all_to_all | solution.py:201
  21.5 10.6 %copy-start.1 = (bf16[1536,768]{1,0:T(8,128)(2,1)S(1)}, bf16[1536,768]{1,0:T(8,128)(2,1)}, u32[]{:S(2)}) copy-start(bf16[1536,768]{1,0:T(8,128)(2,1)} %k_ref.7) | copy-start | bytes 7077892
  21.5 10.6 %copy-start.3 = (bf16[1536,768]{1,0:T(8,128)(2,1)S(1)}, bf16[1536,768]{1,0:T(8,128)(2,1)}, u32[]{:S(2)}) copy-start(bf16[1536,768]{1,0:T(8,128)(2,1)} %v_ref.7) | copy-start | bytes 7077892
  26.0 22.0 %collective-permute-start = (bf16[384,768]{1,0:T(8,128)(2,1)}, bf16[384,768]{1,0:T(8,128)(2,1)}, u32[]{:S(2)}, u32[]{:S(2)}) collective-permute-start(bf16[384,768]{1,0:T(8,128)(2,1)} %get-tuple-element.14), channel_id=1, source_target_pairs={{0,1},{1,2},{2,3},{3,0},{4,5},{5,6},{6,7},{7,4},{8,9},{9,10},{10,1... | collective-permute-start | bytes 1769480 | tf_op jit(solution)/shard_map/ppermute | solution.py:122
  28.2 41.5 %collective-permute-start.1 = (bf16[384,768]{1,0:T(8,128)(2,1)}, bf16[384,768]{1,0:T(8,128)(2,1)}, u32[]{:S(2)}, u32[]{:S(2)}) collective-permute-start(bf16[384,768]{1,0:T(8,128)(2,1)} %get-tuple-element.16), channel_id=1, source_target_pairs={{0,2},{1,3},{2,0},{3,1},{4,6},{5,7},{6,4},{7,5},{8,10},{9,11},{10,... | collective-permute-start | bytes 1769480 | tf_op jit(solution)/shard_map/ppermute | solution.py:122
  30.8 38.9 %collective-permute-start.2 = (bf16[384,768]{1,0:T(8,128)(2,1)S(1)}, bf16[384,768]{1,0:T(8,128)(2,1)}, u32[]{:S(2)}, u32[]{:S(2)}) collective-permute-start(bf16[384,768]{1,0:T(8,128)(2,1)S(1)} %get-tuple-element.15), channel_id=1, source_target_pairs={{0,3},{1,0},{2,1},{3,2},{4,7},{5,4},{6,5},{7,6},{8,11},{9,8},{10,9... | collective-permute-start | bytes 1769480 | tf_op jit(solution)/shard_map/ppermute | solution.py:122
  33.2 1.7 copy-start.14
  42.6 42.3 %all-to-all-start.2 = ((bf16[8,384,512]{2,1,0:T(8,128)(2,1)}), bf16[8,384,512]{2,1,0:T(8,128)(2,1)}, u32[]{:S(2)}, u32[]{:S(2)}) async-start(bf16[8,384,512]{2,1,0:T(8,128)(2,1)} %copy-done.14), calls=%async_computation.2 | async-start | bytes 6291456 | tf_op jit(solution)/shard_map/all_to_all | solution.py:201
  47.1 160.1 %all-gather.5.cloned.1.call-start = ((), (), s32[]{:S(2)}) async-start(), calls=%async_computation.4 | async-start | bytes 1966080 | tf_op jit(solution)/shard_map/all_gather | solution.py:209
  69.7 3.3 %copy-start.4 = (bf16[1536,768]{1,0:T(8,128)(2,1)S(1)}, bf16[1536,768]{1,0:T(8,128)(2,1)}, u32[]{:S(2)}) copy-start(bf16[1536,768]{1,0:T(8,128)(2,1)} %v_ref.7) | copy-start | bytes 7077892
  69.7 3.3 %copy-start.10 = (bf16[1536,768]{1,0:T(8,128)(2,1)S(1)}, bf16[1536,768]{1,0:T(8,128)(2,1)}, u32[]{:S(2)}) copy-start(bf16[1536,768]{1,0:T(8,128)(2,1)} %q_ref.7) | copy-start | bytes 7077892
  81.6 130.9 %all-gather.9.cloned.1.call-start = ((), (), s32[]{:S(2)}) async-start(), calls=%async_computation.6 | async-start | bytes 3932160 | tf_op jit(solution)/shard_map/all_gather | solution.py:209
  85.0 1.7 copy-start.5
  86.7 1.7 copy-start.11
  102.7 154.6 %all-gather.11.cloned.1.call-start = ((), (), s32[]{:S(2)}) async-start(), calls=%async_computation.7 | async-start | bytes 3932160 | tf_op jit(solution)/shard_map/all_gather | solution.py:209
  102.8 1.7 copy-start.6
  105.6 40.6 %copy-start.7 = (bf16[1536,768]{1,0:T(8,128)(2,1)S(1)}, bf16[1536,768]{1,0:T(8,128)(2,1)}, u32[]{:S(2)}) copy-start(bf16[1536,768]{1,0:T(8,128)(2,1)} %v_ref.7) | copy-start | bytes 7077892
  105.6 40.6 %copy-start.12 = (bf16[1536,768]{1,0:T(8,128)(2,1)S(1)}, bf16[1536,768]{1,0:T(8,128)(2,1)}, u32[]{:S(2)}) copy-start(bf16[1536,768]{1,0:T(8,128)(2,1)} %q_ref.7) | copy-start | bytes 7077892
  159.9 41.6 %collective-permute-start.3 = (bf16[4,384,768]{2,1,0:T(8,128)(2,1)}, bf16[4,384,768]{2,1,0:T(8,128)(2,1)}, u32[]{:S(2)}, u32[]{:S(2)}) collective-permute-start(bf16[4,384,768]{2,1,0:T(8,128)(2,1)} %pad_maximum_fusion.1), channel_id=1, source_target_pairs={{0,4},{4,0},{8,12},{12,8},{16,20},{20,16},{24,28},{28,24},{1,5},{5... | collective-permute-start | bytes 7077896 | tf_op jit(solution)/shard_map/ppermute | solution.py:151
  160.0 1.7 copy-start.8
  162.9 1.2 copy-start.15
  164.1 25.4 %all-to-all-start.1 = ((bf16[8,384,256]{2,1,0:T(8,128)(2,1)}), bf16[8,384,256]{2,1,0:T(8,128)(2,1)}, u32[]{:S(2)}, u32[]{:S(2)}) async-start(bf16[8,384,256]{2,1,0:T(8,128)(2,1)} %copy-done.15), calls=%async_computation.1 | async-start | bytes 3145728 | tf_op jit(solution)/shard_map/all_to_all | solution.py:201
  168.4 126.2 %all-gather.7.cloned.1.call-start = ((), (), s32[]{:S(2)}) async-start(), calls=%async_computation.5 | async-start | bytes 1966080 | tf_op jit(solution)/shard_map/all_gather | solution.py:209
  189.4 1.7 copy-start.9
  191.1 1.7 copy-start.13
  257.4 37.2 %copy-start.16 = (bf16[4,128,768]{2,1,0:T(8,128)(2,1)S(1)}, bf16[4,128,768]{2,1,0:T(8,128)(2,1)}, u32[]{:S(2)}) copy-start(bf16[4,128,768]{2,1,0:T(8,128)(2,1)} %get-tuple-element.9) | copy-start | bytes 2359300
Sparse Core Ops, SparseCore 0:
  81.7 47.9 all-gather.4
  131.2 62.2 all-gather.8
  195.2 62.1 all-gather.10
  258.8 35.7 all-gather.6

commit v5 on v3

--- a/solution.py
+++ b/solution.py
@@ -193,9 +193,8 @@
         for start, size in zip(starts, sizes)
     ]
     rows = weight_rows(out_weight)
-    if len(sizes) > 1:
-        rows, outgoing[1] = lax.optimization_barrier((rows, outgoing[1]))
     incoming = [lax.all_to_all(block, "view", 0, 0, tiled=True) for block in outgoing]
+    rows, incoming[0] = lax.optimization_barrier((rows, incoming[0]))
     rows, incoming[-1] = lax.optimization_barrier((rows, incoming[-1]))
     weight = spread_weight(rows)
 

time: 290 us -> 294 us (1.014)
  waiting for transfers between devices: 89.7 us -> 105 us
  Pallas kernels: 45 us -> 37.6 us
  blocking collectives: 48 us -> 41.9 us
  starting transfers between devices: 33.7 us -> 36.8 us
    all_gather x4, waiting for transfers between devices: 14.9 us -> 25.9 us  [local(): gathered = lax.all_gather(attended, 'head', axis=0, tiled=True)]
    all_to_all x3, waiting for transfers between devices: 35.2 us -> 45.3 us  [local(): lax.all_to_all(block, 'view', 0, 0, tiled=True)]
    pallas_call x4, Pallas kernels: 38.3 us -> 31.3 us  [attend(): pl.pallas_call(functools.partial(attend_kernel, slots, tile), grid_spec=p...]
    all_to_all x1, blocking collectives: 48 us -> 41.9 us  [local(): lax.all_to_all(block, 'view', 0, 0, tiled=True)]
    ppermute x10, waiting for transfers between devices: 39.5 us -> 33.9 us  [shift(): lax.ppermute(array, axis, [(i, (i + step) % size) for i in range(size)])]
  transfers between devices with their start and end apart: 17 -> 17, of which waited for: 8 -> 9; matrix products, arithmetic and copies ran while one was open for 8% -> 8% of each run, Pallas kernels for 15% -> 12%
where the time goes in v5:
time: 294 us; the launch traced here: 292 us
  waiting for transfers between devices  105 us (36%)
  blocking collectives  41.9 us (14%)
  Pallas kernels  37.6 us (13%)
  starting transfers between devices  36.8 us (13%)
  local copies, waits for them, and re-layouts  29 us (10%)
  matrix products  27 us (9%)
  between operations  13.4 us (5%)
    all_to_all x3, waiting for transfers between devices, local(): lax.all_to_all(block, 'view', 0, 0, tiled=True)  45.3 us
    all_to_all x1, blocking collectives, local(): lax.all_to_all(block, 'view', 0, 0, tiled=True)  41.9 us
    ppermute x10, waiting for transfers between devices, shift(): lax.ppermute(array, axis, [(i, (i + step) % size) for i in range(size)])  33.9 us
    pallas_call x4, Pallas kernels, attend(): pl.pallas_call(functools.partial(attend_kernel, slots, tile), grid_spec=p...  31.3 us
    dot_general x4, matrix products, local(): lax.dot_general(part.reshape(groups * width, -1), gathered, (((0,), (0,))...  27 us
    all_gather x4, waiting for transfers between devices, local(): gathered = lax.all_gather(attended, 'head', axis=0, tiled=True)  25.9 us
    unnamed x41, local copies, waits for them, and re-layouts  23.9 us
    ppermute x10, starting transfers between devices, shift(): lax.ppermute(array, axis, [(i, (i + step) % size) for i in range(size)])  21.6 us
  transfers between devices with their start and end apart: 17, of which 9 were waited for; matrix products, arithmetic and copies ran while one was open for 8% of the time, Pallas kernels for 12%

profile of v5, /device:TPU:0, one launch (start us, length us, event | category | flops | bytes accessed | tf_op | source)
XLA Modules:
  0.0 292.4 jit_solution(12713861921901982519)
XLA Ops:
  7.3 1.2 dynamic_slice.21
  9.2 1.7 copy-done
  10.9 1.7 copy-done.2
  12.5 1.2 shard_map.64
  13.7 1.1 copy-done.16
  14.9 5.1 %all-to-all-start = ((bf16[8,384,256]{2,1,0:T(8,128)(2,1)}), bf16[8,384,256]{2,1,0:T(8,128)(2,1)}, u32[]{:S(2)}, u32[]{:S(2)}) async-start(bf16[8,384,256]{2,1,0:T(8,128)(2,1)} %copy-done.16), calls=%async_computation | async-start | bytes 3145728 | tf_op jit(solution)/shard_map/all_to_all | solution.py:196
  20.0 1.7 copy-done.3
  21.6 1.1 shard_map.65
  22.8 1.7 copy-done.14
  24.5 16.6 %all-to-all-done.pk_ref.pv_ref = bf16[8,384,256]{2,1,0:T(8,128)(2,1)} async-done(((bf16[8,384,256]{2,1,0:T(8,128)(2,1)}), bf16[8,384,256]{2,1,0:T(8,128)(2,1)}, u32[]{:S(2)}, u32[]{:S(2)}) %all-to-all-start) | async-done | bytes 1572896 | tf_op jit(solution)/shard_map/all_to_all | solution.py:196
  41.1 4.4 %all-to-all-start.1 = ((bf16[8,384,512]{2,1,0:T(8,128)(2,1)}), bf16[8,384,512]{2,1,0:T(8,128)(2,1)}, u32[]{:S(2)}, u32[]{:S(2)}) async-start(bf16[8,384,512]{2,1,0:T(8,128)(2,1)} %copy-done.14), calls=%async_computation.1 | async-start | bytes 6291456 | tf_op jit(solution)/shard_map/all_to_all | solution.py:196
  45.6 1.6 dynamic-slice_bitcast_fusion
  47.2 4.2 %collective-permute-start.2 = (bf16[96,768]{1,0:T(8,128)(2,1)S(1)}, bf16[96,768]{1,0:T(8,128)(2,1)S(1)}, u32[]{:S(2)}, u32[]{:S(2)}) collective-permute-start(bf16[96,768]{1,0:T(8,128)(2,1)S(1)} %get-tuple-element.19), channel_id=1, source_target_pairs={{0,3},{1,0},{2,1},{3,2},{4,7},{5,4},{6,5},{7,6},{8,11},{9,8},{10,9... | collective-permute-start | bytes 442376 | tf_op jit(solution)/shard_map/ppermute | solution.py:122
  53.1 2.6 collective-permute-done.2
  55.7 8.7 %collective-permute-done.1 = bf16[96,768]{1,0:T(8,128)(2,1)S(1)} collective-permute-done((bf16[96,768]{1,0:T(8,128)(2,1)S(1)}, bf16[96,768]{1,0:T(8,128)(2,1)S(1)}, u32[]{:S(2)}, u32[]{:S(2)}) %collective-permute-start.1) | collective-permute-done | bytes 147488 | tf_op jit(solution)/shard_map/ppermute | solution.py:122
  64.5 1.7 copy-done.4
  66.1 1.7 copy-done.10
  67.8 6.3 %shard_map.67 = bf16[128,1536]{1,0:T(8,128)(2,1)} custom-call(s32[15]{0:T(128)S(1)} %pad_add_fusion.1.meta_ref, bf16[1536,768]{1,0:T(8,128)(2,1)S(1)} %copy-done.10, bf16[1536,768]{1,0:T(8,128)(2,1)S(1)} %copy-done.1, bf16[1536,768]{1,0:T(8,128)(2,1)S(1)} %copy-done.4, bf16[8,384,256]{2,1,0:T(8,128)(2,1)} %all-to-all-done.pk_ref.pv_ref, ...), custom_call_target="tpu_custom_call" | custom-call | flops 1660944384 | bytes 3145728 | tf_op jit(solution)/shard_map/pallas_call | solution.py:97
  74.1 9.3 %all-to-all-done.1.pk_ref.pv_ref = bf16[8,384,512]{2,1,0:T(8,128)(2,1)} async-done(((bf16[8,384,512]{2,1,0:T(8,128)(2,1)}), bf16[8,384,512]{2,1,0:T(8,128)(2,1)}, u32[]{:S(2)}, u32[]{:S(2)}) %all-to-all-start.1) | async-done | bytes 3145760 | tf_op jit(solution)/shard_map/all_to_all | solution.py:196
  83.5 1.7 copy-done.5
  85.1 1.7 copy-done.11
  86.8 9.7 %shard_map.72 = bf16[256,1536]{1,0:T(8,128)(2,1)} custom-call(s32[15]{0:T(128)S(1)} %pad_add_fusion.1.meta_ref, bf16[1536,768]{1,0:T(8,128)(2,1)S(1)} %copy-done.11, bf16[1536,768]{1,0:T(8,128)(2,1)S(1)} %copy-done.1, bf16[1536,768]{1,0:T(8,128)(2,1)S(1)} %copy-done.5, bf16[8,384,512]{2,1,0:T(8,128)(2,1)} %all-to-all-done.1.pk_ref.pv_ref, ...), custom_call_target="tpu_custom_call" | custom-call | flops 3321888768 | bytes 6291456 | tf_op jit(solution)/shard_map/pallas_call | solution.py:97
  96.6 1.7 copy-done.6
  98.3 1.1 shard_map.70
  99.4 41.9 %all_to_all.20.pk_ref.pv_ref = bf16[8,384,512]{2,1,0:T(8,128)(2,1)S(1)} all-to-all(bf16[8,384,512]{2,1,0:T(8,128)(2,1)S(1)} %shard_map.70), channel_id=1, replica_groups=mesh['view'=8,'head'=4] {'view'}, dimensions={0} | all-to-all | bytes 6291456 | tf_op jit(solution)/shard_map/all_to_all | solution.py:196
  141.4 9.1 %shard_map.71 = bf16[256,1536]{1,0:T(8,128)(2,1)} custom-call(s32[15]{0:T(128)S(1)} %pad_add_fusion.1.meta_ref, bf16[1536,768]{1,0:T(8,128)(2,1)S(1)} %copy-done.12, bf16[1536,768]{1,0:T(8,128)(2,1)S(1)} %copy-done.1, bf16[1536,768]{1,0:T(8,128)(2,1)S(1)} %copy-done.7, bf16[8,384,512]{2,1,0:T(8,128)(2,1)S(1)} %all_to_all.20.pk_ref.pv_ref, ...), custom_call_target="tpu_custom_call" | custom-call | flops 3321888768 | bytes 6291456 | tf_op jit(solution)/shard_map/pallas_call | solution.py:97
  150.5 1.7 copy-done.8
  152.2 1.2 shard_map.68
  153.4 1.1 copy-done.15
  154.5 5.5 %all-to-all-start.2 = ((bf16[8,384,256]{2,1,0:T(8,128)(2,1)}), bf16[8,384,256]{2,1,0:T(8,128)(2,1)}, u32[]{:S(2)}, u32[]{:S(2)}) async-start(bf16[8,384,256]{2,1,0:T(8,128)(2,1)} %copy-done.15), calls=%async_computation.2 | async-start | bytes 3145728 | tf_op jit(solution)/shard_map/all_to_all | solution.py:196
  160.6 1.7 collective-permute-start.4
  162.2 19.4 %all-to-all-done.2.pk_ref.pv_ref = bf16[8,384,256]{2,1,0:T(8,128)(2,1)} async-done(((bf16[8,384,256]{2,1,0:T(8,128)(2,1)}), bf16[8,384,256]{2,1,0:T(8,128)(2,1)}, u32[]{:S(2)}, u32[]{:S(2)}) %all-to-all-start.2) | async-done | bytes 1572896 | tf_op jit(solution)/shard_map/all_to_all | solution.py:196
  181.6 1.8 copy-done.9
  183.4 1.9 copy-done.13
  185.2 6.2 %shard_map.69 = bf16[128,1536]{1,0:T(8,128)(2,1)} custom-call(s32[15]{0:T(128)S(1)} %pad_add_fusion.1.meta_ref, bf16[1536,768]{1,0:T(8,128)(2,1)S(1)} %copy-done.13, bf16[1536,768]{1,0:T(8,128)(2,1)S(1)} %copy-done.1, bf16[1536,768]{1,0:T(8,128)(2,1)S(1)} %copy-done.9, bf16[8,384,256]{2,1,0:T(8,128)(2,1)} %all-to-all-done.2.pk_ref.pv_ref, ...), custom_call_target="tpu_custom_call" | custom-call | flops 1660944384 | bytes 3145728 | tf_op jit(solution)/shard_map/pallas_call | solution.py:97
  192.2 1.4 collective-permute-start.7
  193.6 2.2 collective-permute-start.8
  195.8 1.1 bitcast_dynamic-update-slice_fusion.6
  196.9 10.0 %collective-permute-start.9 = (bf16[4,96,768]{2,1,0:T(8,128)(2,1)S(1)}, bf16[4,96,768]{2,1,0:T(8,128)(2,1)S(1)}, u32[]{:S(2)}, u32[]{:S(2)}) collective-permute-start(bf16[4,96,768]{2,1,0:T(8,128)(2,1)S(1)} %pad_maximum_fusion), channel_id=1, source_target_pairs={{0,28},{4,0},{8,4},{12,8},{16,12},{20,16},{24,20},{28,24},{1,29},{... | collective-permute-start | bytes 1769480 | tf_op jit(solution)/shard_map/ppermute | solution.py:122
  207.0 11.9 %collective-permute-done.5 = bf16[4,96,768]{2,1,0:T(8,128)(2,1)S(1)} collective-permute-done((bf16[4,96,768]{2,1,0:T(8,128)(2,1)S(1)}, bf16[4,96,768]{2,1,0:T(8,128)(2,1)S(1)}, u32[]{:S(2)}, u32[]{:S(2)}) %collective-permute-start.5) | collective-permute-done | bytes 589856 | tf_op jit(solution)/shard_map/ppermute | solution.py:122
  219.0 10.6 %collective-permute-done.7 = bf16[4,96,768]{2,1,0:T(8,128)(2,1)S(1)} collective-permute-done((bf16[4,96,768]{2,1,0:T(8,128)(2,1)S(1)}, bf16[4,96,768]{2,1,0:T(8,128)(2,1)S(1)}, u32[]{:S(2)}, u32[]{:S(2)}) %collective-permute-start.7) | collective-permute-done | bytes 589856 | tf_op jit(solution)/shard_map/ppermute | solution.py:122
  229.8 1.6 shard_map.66
  231.6 1.4 fusion.2
  232.9 5.0 %fusion.3 = f32[768,1536]{1,0:T(8,128)} fusion(bf16[512,768]{1,0:T(8,128)(2,1)S(1)} %bitcast.47, bf16[512,1536]{1,0:T(8,128)(2,1)} %all-gather.5.cloned.1.call-done), kind=kOutput, calls=%fused_computation.21 | convolution fusion | flops 1207959552 | bytes 7077888 | tf_op jit(solution)/shard_map/dot_general | solution.py:207
  237.9 7.2 %fusion.5 = f32[768,1536]{1,0:T(8,128)} fusion(bf16[1024,768]{1,0:T(8,128)(2,1)} %bitcast.45, bf16[1024,1536]{1,0:T(8,128)(2,1)} %all-gather.11.cloned.1.call-done), kind=kOutput, calls=%fused_computation.23 | convolution fusion | flops 2415919104 | bytes 9437184 | tf_op jit(solution)/shard_map/dot_general | solution.py:207
  245.1 6.2 %fusion.4 = f32[768,1536]{1,0:T(8,128)} fusion(bf16[1024,768]{1,0:T(8,128)(2,1)S(1)} %bitcast.44, bf16[1024,1536]{1,0:T(8,128)(2,1)} %all-gather.9.cloned.1.call-done), kind=kOutput, calls=%fused_computation.22 | convolution fusion | flops 2415919104 | bytes 9437184 | tf_op jit(solution)/shard_map/dot_general | solution.py:207
  251.3 25.9 %all-gather.7.cloned.1.call-done = bf16[512,1536]{1,0:T(8,128)(2,1)} async-done(((bf16[128,1536]{1,0:T(8,128)(2,1)}), bf16[512,1536]{1,0:T(8,128)(2,1)}) %all-gather.7.cloned.1.call-update) | async-done | bytes 1572880 | tf_op jit(solution)/shard_map/all_gather | solution.py:205
  277.3 8.6 %add_convert_fusion = bf16[768,1536]{1,0:T(8,128)(2,1)} fusion(f32[768,1536]{1,0:T(8,128)} %fusion.5, f32[768,1536]{1,0:T(8,128)} %fusion.4, f32[768,1536]{1,0:T(8,128)} %fusion.3, bf16[512,768]{1,0:T(8,128)(2,1)S(1)} %bitcast.46, bf16[512,1536]{1,0:T(8,128)(2,1)} %all-gather.7.cloned.1.call-done), kind=kOutput, calls=%fused_computation | convolution fusion | flops 1212678144 | bytes 18874368 | tf_op jit(solution)/shard_map/dot_general | solution.py:207
  (56 shorter events, 5.1 us)
Async XLA Ops:
  9.2 1.7 copy-start
  10.8 1.7 copy-start.2
  12.5 7.5 %copy-start.1 = (bf16[1536,768]{1,0:T(8,128)(2,1)S(1)}, bf16[1536,768]{1,0:T(8,128)(2,1)}, u32[]{:S(2)}) copy-start(bf16[1536,768]{1,0:T(8,128)(2,1)} %k_ref.7) | copy-start | bytes 7077892
  13.7 1.1 copy-start.16
  14.9 26.2 %all-to-all-start = ((bf16[8,384,256]{2,1,0:T(8,128)(2,1)}), bf16[8,384,256]{2,1,0:T(8,128)(2,1)}, u32[]{:S(2)}, u32[]{:S(2)}) async-start(bf16[8,384,256]{2,1,0:T(8,128)(2,1)} %copy-done.16), calls=%async_computation | async-start | bytes 3145728 | tf_op jit(solution)/shard_map/all_to_all | solution.py:196
  20.0 1.7 copy-start.3
  22.8 1.7 copy-start.14
  41.1 42.3 %all-to-all-start.1 = ((bf16[8,384,512]{2,1,0:T(8,128)(2,1)}), bf16[8,384,512]{2,1,0:T(8,128)(2,1)}, u32[]{:S(2)}, u32[]{:S(2)}) async-start(bf16[8,384,512]{2,1,0:T(8,128)(2,1)} %copy-done.14), calls=%async_computation.1 | async-start | bytes 6291456 | tf_op jit(solution)/shard_map/all_to_all | solution.py:196
  45.6 187.4 %all-gather.5.cloned.1.call-start = ((), (), s32[]{:S(2)}) async-start(), calls=%async_computation.4 | async-start | bytes 1966080 | tf_op jit(solution)/shard_map/all_gather | solution.py:205
  47.2 8.5 %collective-permute-start.2 = (bf16[96,768]{1,0:T(8,128)(2,1)S(1)}, bf16[96,768]{1,0:T(8,128)(2,1)S(1)}, u32[]{:S(2)}, u32[]{:S(2)}) collective-permute-start(bf16[96,768]{1,0:T(8,128)(2,1)S(1)} %get-tuple-element.19), channel_id=1, source_target_pairs={{0,3},{1,0},{2,1},{3,2},{4,7},{5,4},{6,5},{7,6},{8,11},{9,8},{10,9... | collective-permute-start | bytes 442376 | tf_op jit(solution)/shard_map/ppermute | solution.py:122
  51.4 13.0 %collective-permute-start.1 = (bf16[96,768]{1,0:T(8,128)(2,1)S(1)}, bf16[96,768]{1,0:T(8,128)(2,1)S(1)}, u32[]{:S(2)}, u32[]{:S(2)}) collective-permute-start(bf16[96,768]{1,0:T(8,128)(2,1)S(1)} %get-tuple-element.20), channel_id=1, source_target_pairs={{0,2},{1,3},{2,0},{3,1},{4,6},{5,7},{6,4},{7,5},{8,10},{9,11},{10,... | collective-permute-start | bytes 442376 | tf_op jit(solution)/shard_map/ppermute | solution.py:122
  51.4 13.0 %collective-permute-start = (bf16[96,768]{1,0:T(8,128)(2,1)S(1)}, bf16[96,768]{1,0:T(8,128)(2,1)S(1)}, u32[]{:S(2)}, u32[]{:S(2)}) collective-permute-start(bf16[96,768]{1,0:T(8,128)(2,1)S(1)} %get-tuple-element.18), channel_id=1, source_target_pairs={{0,1},{1,2},{2,3},{3,0},{4,5},{5,6},{6,7},{7,4},{8,9},{9,10},{10,1... | collective-permute-start | bytes 442376 | tf_op jit(solution)/shard_map/ppermute | solution.py:122
  64.5 1.7 copy-start.4
  66.1 1.7 copy-start.10
  74.1 163.8 %all-gather.11.cloned.1.call-start = ((), (), s32[]{:S(2)}) async-start(), calls=%async_computation.7 | async-start | bytes 3932160 | tf_op jit(solution)/shard_map/all_gather | solution.py:205
  83.4 1.7 copy-start.5
  85.1 1.7 copy-start.11
  96.5 148.5 %all-gather.9.cloned.1.call-start = ((), (), s32[]{:S(2)}) async-start(), calls=%async_computation.6 | async-start | bytes 3932160 | tf_op jit(solution)/shard_map/all_gather | solution.py:205
  96.6 1.7 copy-start.6
  99.4 42.0 %copy-start.7 = (bf16[1536,768]{1,0:T(8,128)(2,1)S(1)}, bf16[1536,768]{1,0:T(8,128)(2,1)}, u32[]{:S(2)}) copy-start(bf16[1536,768]{1,0:T(8,128)(2,1)} %v_ref.7) | copy-start | bytes 7077892
  99.4 42.0 %copy-start.12 = (bf16[1536,768]{1,0:T(8,128)(2,1)S(1)}, bf16[1536,768]{1,0:T(8,128)(2,1)}, u32[]{:S(2)}) copy-start(bf16[1536,768]{1,0:T(8,128)(2,1)} %q_ref.7) | copy-start | bytes 7077892
  150.5 1.7 copy-start.8
  153.4 1.1 copy-start.15
  154.5 27.1 %all-to-all-start.2 = ((bf16[8,384,256]{2,1,0:T(8,128)(2,1)}), bf16[8,384,256]{2,1,0:T(8,128)(2,1)}, u32[]{:S(2)}, u32[]{:S(2)}) async-start(bf16[8,384,256]{2,1,0:T(8,128)(2,1)} %copy-done.15), calls=%async_computation.2 | async-start | bytes 3145728 | tf_op jit(solution)/shard_map/all_to_all | solution.py:196
  160.0 117.3 %all-gather.7.cloned.1.call-start = ((), (), s32[]{:S(2)}) async-start(), calls=%async_computation.5 | async-start | bytes 1966080 | tf_op jit(solution)/shard_map/all_gather | solution.py:205
  160.0 33.6 %collective-permute-start.3 = (bf16[4,96,768]{2,1,0:T(8,128)(2,1)S(1)}, bf16[4,96,768]{2,1,0:T(8,128)(2,1)}, u32[]{:S(2)}, u32[]{:S(2)}) collective-permute-start(bf16[4,96,768]{2,1,0:T(8,128)(2,1)S(1)} %pad_maximum_fusion), channel_id=1, source_target_pairs={{0,4},{4,8},{8,12},{12,16},{16,20},{20,24},{24,28},{28,0},{1,5},{5... | collective-permute-start | bytes 1769480 | tf_op jit(solution)/shard_map/ppermute | solution.py:122
  160.6 36.3 %collective-permute-start.4 = (bf16[4,96,768]{2,1,0:T(8,128)(2,1)S(1)}, bf16[4,96,768]{2,1,0:T(8,128)(2,1)S(1)}, u32[]{:S(2)}, u32[]{:S(2)}) collective-permute-start(bf16[4,96,768]{2,1,0:T(8,128)(2,1)S(1)} %pad_maximum_fusion), channel_id=1, source_target_pairs={{0,8},{4,12},{8,16},{12,20},{16,24},{20,28},{24,0},{28,4},{1,9},{5... | collective-permute-start | bytes 1769480 | tf_op jit(solution)/shard_map/ppermute | solution.py:122
  181.6 1.8 copy-start.9
  183.4 1.9 copy-start.13
  191.5 27.4 %collective-permute-start.5 = (bf16[4,96,768]{2,1,0:T(8,128)(2,1)S(1)}, bf16[4,96,768]{2,1,0:T(8,128)(2,1)S(1)}, u32[]{:S(2)}, u32[]{:S(2)}) collective-permute-start(bf16[4,96,768]{2,1,0:T(8,128)(2,1)S(1)} %pad_maximum_fusion), channel_id=1, source_target_pairs={{0,12},{4,16},{8,20},{12,24},{16,28},{20,0},{24,4},{28,8},{1,13},{... | collective-permute-start | bytes 1769480 | tf_op jit(solution)/shard_map/ppermute | solution.py:122
  191.6 27.4 %collective-permute-start.6 = (bf16[4,96,768]{2,1,0:T(8,128)(2,1)S(1)}, bf16[4,96,768]{2,1,0:T(8,128)(2,1)S(1)}, u32[]{:S(2)}, u32[]{:S(2)}) collective-permute-start(bf16[4,96,768]{2,1,0:T(8,128)(2,1)S(1)} %pad_maximum_fusion), channel_id=1, source_target_pairs={{0,16},{4,20},{8,24},{12,28},{16,0},{20,4},{24,8},{28,12},{1,17},{... | collective-permute-start | bytes 1769480 | tf_op jit(solution)/shard_map/ppermute | solution.py:122
  192.2 37.5 %collective-permute-start.7 = (bf16[4,96,768]{2,1,0:T(8,128)(2,1)S(1)}, bf16[4,96,768]{2,1,0:T(8,128)(2,1)S(1)}, u32[]{:S(2)}, u32[]{:S(2)}) collective-permute-start(bf16[4,96,768]{2,1,0:T(8,128)(2,1)S(1)} %pad_maximum_fusion), channel_id=1, source_target_pairs={{0,20},{4,24},{8,28},{12,0},{16,4},{20,8},{24,12},{28,16},{1,21},{... | collective-permute-start | bytes 1769480 | tf_op jit(solution)/shard_map/ppermute | solution.py:122
  193.6 36.1 %collective-permute-start.8 = (bf16[4,96,768]{2,1,0:T(8,128)(2,1)S(1)}, bf16[4,96,768]{2,1,0:T(8,128)(2,1)S(1)}, u32[]{:S(2)}, u32[]{:S(2)}) collective-permute-start(bf16[4,96,768]{2,1,0:T(8,128)(2,1)S(1)} %pad_maximum_fusion), channel_id=1, source_target_pairs={{0,24},{4,28},{8,0},{12,4},{16,8},{20,12},{24,16},{28,20},{1,25},{... | collective-permute-start | bytes 1769480 | tf_op jit(solution)/shard_map/ppermute | solution.py:122
  196.9 32.9 %collective-permute-start.9 = (bf16[4,96,768]{2,1,0:T(8,128)(2,1)S(1)}, bf16[4,96,768]{2,1,0:T(8,128)(2,1)S(1)}, u32[]{:S(2)}, u32[]{:S(2)}) collective-permute-start(bf16[4,96,768]{2,1,0:T(8,128)(2,1)S(1)} %pad_maximum_fusion), channel_id=1, source_target_pairs={{0,28},{4,0},{8,4},{12,8},{16,12},{20,16},{24,20},{28,24},{1,29},{... | collective-permute-start | bytes 1769480 | tf_op jit(solution)/shard_map/ppermute | solution.py:122
Sparse Core Ops, SparseCore 0:
  74.2 38.0 all-gather.4
  113.9 62.3 all-gather.10
  177.9 62.1 all-gather.8
  241.5 35.7 all-gather.6
